TPU v7x, 32 devices: a whole 2x2x4 slice. The times are simulated.
32 devices in a mesh: edata: 16 (over z, y, x), llm: 2 (over core).
Axes of the slice: x: 2, y: 2, z: 4, core: 2. Of those that a mesh axis runs over, the one named last changes fastest.
Arguments:
- grad_rows: bfloat16 [2048, 3200], P(('edata', 'llm')), may hold values from -6 to 6
- row_target: int32 [2048, 1], P(('edata', 'llm')), may hold values from 0 to 15; in each aligned block of 64 rows (0 to 63, 64 to 127, ...) at most 5 rows name the same one
- stored_context: bfloat16 [2560, 2048], P('edata', 'llm'), may hold values from -448 to 448
- block_scale: float32 [2560, 16], P('edata', 'llm'), may hold values from 0.002 to 0.008
- w_out: bfloat16 [2048, 3200], P('llm', 'edata'), may hold values from -0.125 to 0.125
- layer_scale: float32 [3200], replicated, may hold values from 0.3 to 3
Outputs:
- grad_context: bfloat16 [2560, 2048], P('edata', 'llm')
- grad_weight: float32 [3200, 2048], P('edata', 'llm')
- grad_scale: float32 [3200], replicated
Inputs may be any that keep to these rules, and one draw needn't show every extreme that they name: `row_target`: among the 64 rows of one device, no encoder device is named by more than 5 rows, and some encoder device is named by exactly 5 rows.
All inputs are finite; a program needn't handle non-finite values.
Results may differ from a plain program's by a relative error of at most 0.0049.
Values may be sent and summed in bfloat16 or wider, within the bound.
A program may use at most 128 MiB of HBM per device.

v0:
```python
import math

import jax
import jax.numpy as jnp
from jax import lax
from jax.sharding import PartitionSpec as P

BLOCK = 128


def on_device(grad_rows, row_target, stored_context, block_scale, w_out, layer_scale):
    encoders = lax.axis_size("edata")
    owners = lax.axis_size("llm")
    source_rows = grad_rows.shape[0]
    features = grad_rows.shape[1]
    slot_count = stored_context.shape[0]
    capacity = slot_count // (encoders * owners)
    weights = lax.all_gather(w_out, "edata", axis=1, tiled=True)
    targets = row_target[:, 0]
    chosen = (targets[:, None] == jnp.arange(encoders, dtype=jnp.int32)[None, :]).astype(jnp.int32)
    arrival = jnp.sum(chosen * (jnp.cumsum(chosen, axis=0) - 1), axis=1)
    position = targets * capacity + arrival
    outgoing = jnp.zeros((encoders * capacity, features), jnp.bfloat16).at[position].set(grad_rows)
    arrived = lax.all_to_all(outgoing, "edata", split_axis=0, concat_axis=0, tiled=True)
    grad_slots = lax.all_gather(arrived, "llm", axis=0, tiled=True)
    stored = stored_context.astype(jnp.float32).reshape(slot_count, -1, BLOCK)
    context = (stored * block_scale[:, :, None]).reshape(slot_count, -1).astype(jnp.bfloat16)
    scaled = (grad_slots.astype(jnp.float32) * layer_scale[None, :]).astype(jnp.bfloat16)
    recomputed = jnp.dot(context, weights, preferred_element_type=jnp.float32)
    grad_context = lax.dot_general(
        scaled, weights, (((1,), (1,)), ((), ())), preferred_element_type=jnp.float32
    ).astype(jnp.bfloat16)
    partial_scale = jnp.sum(grad_slots.astype(jnp.float32) * recomputed, axis=0)
    rescale = 1.0 / math.sqrt(source_rows * encoders * owners)
    grad_weight = (
        lax.psum_scatter(
            lax.dot_general(
                scaled, context, (((0,), (0,)), ((), ())), preferred_element_type=jnp.float32
            ),
            "edata",
            scatter_dimension=0,
            tiled=True,
        )
        * rescale
    )
    grad_scale = lax.psum(partial_scale, ("edata", "llm")) * rescale
    return (grad_context, grad_weight, grad_scale)


def solution(mesh):
    in_specs = (
        P(("edata", "llm"), None),
        P(("edata", "llm"), None),
        P("edata", "llm"),
        P("edata", "llm"),
        P("llm", "edata"),
        P(),
    )
    out_specs = (P("edata", "llm"), P("edata", "llm"), P())
    return jax.shard_map(
        on_device, mesh=mesh, in_specs=in_specs, out_specs=out_specs, check_vma=False
    )
```

profile of v0, /device:TPU:0, one launch (start us, length us, event | category | flops | bytes accessed | tf_op | source)
XLA Modules:
  0.0 404.3 jit_solution(17853979694073448699)
XLA Ops:
  7.2 0.0 copy-start.1
  7.2 0.0 copy-start
  7.2 0.0 all-gather.2.cloned.1.call-start
  7.2 0.7 all-gather.2.cloned.1.call-update
  7.9 0.7 fusion.8
  8.6 0.1 reduce_window_sum.11
  8.7 0.8 select_reduce_fusion
  9.6 0.7 fusion.9
  10.3 1.8 scatter_custom_fusion
  12.0 1.1 all_to_all.8
  13.1 8.3 %all-to-all-start = ((bf16[16,5,3200]{2,1,0:T(8,128)(2,1)}), bf16[16,5,3200]{2,1,0:T(8,128)(2,1)S(1)}, u32[]{:S(2)}, u32[]{:S(2)}) async-start(bf16[16,5,3200]{2,1,0:T(8,128)(2,1)} %all_to_all.8), calls=%async_computation | async-start | bytes 1638400 | tf_op jit(solution)/shard_map/all_to_all | solution.py:24
  21.4 0.0 reduce-scatter.2.cloned.1.call-start
  21.5 0.8 copy.10
  22.3 28.2 %all-to-all-done = bf16[16,5,3200]{2,1,0:T(8,128)(2,1)S(1)} async-done(((bf16[16,5,3200]{2,1,0:T(8,128)(2,1)}), bf16[16,5,3200]{2,1,0:T(8,128)(2,1)S(1)}, u32[]{:S(2)}, u32[]{:S(2)}) %all-to-all-start) | async-done | bytes 512032 | tf_op jit(solution)/shard_map/all_to_all | solution.py:24
  50.5 0.2 all_to_all.10
  50.7 2.5 all_gather.6
  53.3 0.2 mul.49
  53.5 0.0 copy-done.1
  53.5 0.0 copy-done
  53.5 6.6 %fusion.2 = f32[3200,1024]{1,0:T(8,128)} fusion(bf16[160,3200]{1,0:T(8,128)(2,1)S(1)} %all_gather.6, f32[3200]{0:T(1024)S(1)} %copy-done.1, f32[20,8,8,128]{3,2,1,0:T(8,128)S(1)} %bitcast.17, bf16[160,1024]{1,0:T(8,128)(2,1)S(1)} %copy-done), kind=kOutput, calls=%fused_computation.6 | convolution fusion | flops 1050603520 | bytes 15127040 | tf_op jit(solution)/shard_map/dot_general | solution.py:37
  60.1 0.0 reduce-scatter.2.cloned.1.call-update
  60.1 60.6 %all-gather.2.cloned.1.call-done = bf16[1024,3200]{0,1:T(8,128)(2,1)} async-done(((bf16[1024,200]{0,1:T(8,128)(2,1)}), bf16[1024,3200]{0,1:T(8,128)(2,1)}) %all-gather.2.cloned.1.call-update) | async-done | bytes 6553616 | tf_op jit(solution)/shard_map/all_gather | solution.py:18
  120.8 5.2 %fusion.1 = f32[3200]{0:T(1024)S(1)} fusion(bf16[1024,3200]{0,1:T(8,128)(2,1)} %all-gather.2.cloned.1.call-done, bf16[160,3200]{1,0:T(8,128)(2,1)S(1)} %all_gather.6, f32[20,8,8,128]{3,2,1,0:T(8,128)S(1)} %bitcast.18, bf16[160,1024]{1,0:T(8,128)(2,1)S(1)} %copy-done), kind=kOutput, calls=%fused_computation.4 | convolution fusion | flops 1050600320 | bytes 8573440 | tf_op jit(solution)/shard_map/dot_general | solution.py:29
  125.9 57.4 %psum.7 = f32[3200]{0:T(1024)S(1)} all-reduce(f32[3200]{0:T(1024)S(1)} %fusion.1), channel_id=1, replica_groups=mesh['edata'=16,'llm'=2] {'edata','llm'}, use_global_device_ids=true, to_apply=%region_5.6 | all-reduce | flops 3200 | bytes 25600 | tf_op jit(solution)/shard_map/psum | solution.py:46
  183.4 0.6 broadcast_multiply_fusion.1
  184.0 4.9 %convolution_convert_fusion = bf16[160,1024]{1,0:T(8,128)(2,1)} fusion(bf16[1024,3200]{0,1:T(8,128)(2,1)} %all-gather.2.cloned.1.call-done, bf16[160,3200]{1,0:T(8,128)(2,1)S(1)} %all_gather.6, f32[3200]{0:T(1024)S(1)} %copy-done.1), kind=kOutput, calls=%fused_computation.5 | convolution fusion | flops 1050275840 | bytes 7918080 | tf_op jit(solution)/shard_map/dot_general | solution.py:30
  188.9 206.4 %reduce-scatter.2.cloned.1.call-done = f32[200,1024]{1,0:T(8,128)} async-done(((f32[3200,1024]{1,0:T(8,128)}), f32[200,1024]{1,0:T(8,128)}) %reduce-scatter.2.cloned.1.call-update) | async-done | bytes 819216 | tf_op jit(solution)/shard_map/reduce_scatter | solution.py:36
  395.3 2.1 broadcast_multiply_fusion
Async XLA Ops:
  7.2 46.3 %copy-start.1 = (f32[3200]{0:T(1024)S(1)}, f32[3200]{0:T(1024)}, u32[]{:S(2)}) copy-start(f32[3200]{0:T(1024)} %param.11) | copy-start | bytes 38404
  7.2 46.3 %copy-start = (bf16[160,1024]{1,0:T(8,128)(2,1)S(1)}, bf16[160,1024]{1,0:T(8,128)(2,1)}, u32[]{:S(2)}) copy-start(bf16[160,1024]{1,0:T(8,128)(2,1)} %param.8) | copy-start | bytes 983044
  7.2 113.6 %all-gather.2.cloned.1.call-start = ((), (), s32[]{:S(2)}) async-start(), calls=%async_computation.2 | async-start | bytes 6963200 | tf_op jit(solution)/shard_map/all_gather | solution.py:18
  13.1 37.4 %all-to-all-start = ((bf16[16,5,3200]{2,1,0:T(8,128)(2,1)}), bf16[16,5,3200]{2,1,0:T(8,128)(2,1)S(1)}, u32[]{:S(2)}, u32[]{:S(2)}) async-start(bf16[16,5,3200]{2,1,0:T(8,128)(2,1)} %all_to_all.8), calls=%async_computation | async-start | bytes 1638400 | tf_op jit(solution)/shard_map/all_to_all | solution.py:24
  21.4 373.9 %reduce-scatter.2.cloned.1.call-start = ((), (), s32[]{:S(2)}) async-start(), calls=%async_computation.3 | async-start | bytes 13926400 | tf_op jit(solution)/shard_map/reduce_scatter | solution.py:36
Sparse Core Ops, SparseCore 0:
  10.7 110.0 all-gather.1
  123.1 272.1 reduce-scatter.1
where the time goes:
time: 408 us; the launch traced here: 404 us
  waiting for transfers between devices  296 us (73%)
  blocking collectives  60 us (15%)
  matrix products  16.6 us (4%)
  between operations  14.1 us (3%)
  starting transfers between devices  8.39 us (2%)
  other arithmetic  5.08 us (1%)
  local copies, waits for them, and re-layouts  4.12 us (1%)
    reduce_scatter x1, waiting for transfers between devices, on_device(): lax.psum_scatter(lax.dot_general(scaled, context, (((0,), (0,)), ((), ())...  206 us
    all_gather x1, waiting for transfers between devices, on_device(): weights = lax.all_gather(w_out, 'edata', axis=1, tiled=True)  60.6 us
    psum x1, blocking collectives, on_device(): grad_scale = lax.psum(partial_scale, ('edata', 'llm')) * rescale  57.4 us
    all_to_all x1, waiting for transfers between devices, on_device(): lax.all_to_all(outgoing, 'edata', split_axis=0, concat_axis=0, tiled=True)  28.2 us
    all_to_all x1, starting transfers between devices, on_device(): lax.all_to_all(outgoing, 'edata', split_axis=0, concat_axis=0, tiled=True)  8.31 us
  transfers between devices with their start and end apart: 3, of which 3 were waited for; matrix products, arithmetic and copies ran while one was open for 6% of the time, Pallas kernels for 0%

commit v1 on v0

--- a/solution.py
+++ b/solution.py
@@ -1,11 +1,319 @@
+import functools
 import math
 
 import jax
 import jax.numpy as jnp
 from jax import lax
+from jax.experimental import pallas as pl
+from jax.experimental.pallas import tpu as pltpu
 from jax.sharding import PartitionSpec as P
 
 BLOCK = 128
+GROUP = 4
+MESH = pl.DeviceIdType.MESH
+
+
+def up(value, unit):
+    return -(-value // unit) * unit
+
+
+def kernel(
+    capacity, rescale, rows_ref, place_ref, context_ref, weight_ref,
+    grad_context_ref, grad_weight_ref, scale_ref,
+    row_buf, place_buf, routed, arrived, grads, grads_t, contexts, weights,
+    context_out, context_in, weight_out, weight_in, scale_pair, scale_group,
+    row_send, row_recv, place_send, place_recv, context_send, context_recv,
+    weight_send, weight_recv, routed_send, routed_recv, gc_send, gc_recv,
+    gw_send, gw_recv, pair_send, pair_recv, group_send, group_recv, all_send, all_recv,
+):
+    e, core = lax.axis_index("edata"), lax.axis_index("llm")
+    depth, plane = e // GROUP, e % GROUP
+    other = 1 - core
+    features = weight_ref.shape[0]
+    slots = context_ref.shape[0]
+    block = routed.shape[1]
+
+    def ahead(own, k):
+        return (own + k) % GROUP
+
+    def along_depth(k):
+        return (ahead(depth, k) * GROUP + plane, core)
+
+    def along_plane(k, owner):
+        return (depth * GROUP + ahead(plane, k), owner)
+
+    def send(src, dst, send_sem, recv_sem, device):
+        return pltpu.make_async_remote_copy(
+            src_ref=src, dst_ref=dst, send_sem=send_sem, recv_sem=recv_sem,
+            device_id=device, device_id_type=MESH,
+        )
+
+    barrier = pltpu.get_barrier_semaphore()
+    for k in range(1, GROUP):
+        pl.semaphore_signal(barrier, inc=1, device_id=along_depth(k), device_id_type=MESH)
+        for owner in (core, other):
+            pl.semaphore_signal(
+                barrier, inc=1, device_id=along_plane(k, owner), device_id_type=MESH
+            )
+    pl.semaphore_signal(barrier, inc=1, device_id=(e, other), device_id_type=MESH)
+    pl.semaphore_wait(barrier, 3 * (GROUP - 1) + 1)
+
+    row_copies = []
+    place_copies = []
+    for k in range(1, GROUP):
+        row_copies.append(
+            send(rows_ref.at[ahead(depth, k)], row_buf.at[depth],
+                 row_send.at[k - 1], row_recv.at[k - 1], along_depth(k))
+        )
+        place_copies.append(
+            send(place_ref, place_buf.at[depth],
+                 place_send.at[k - 1], place_recv.at[k - 1], along_depth(k))
+        )
+    for copy in place_copies + row_copies:
+        copy.start()
+    weight_copies = [
+        send(weight_ref, weights.at[plane], weight_send.at[k - 1], weight_recv.at[k - 1],
+             along_plane(k, core))
+        for k in range(1, GROUP)
+    ]
+    for copy in weight_copies:
+        copy.start()
+    context_copies = [
+        send(context_ref, contexts.at[depth], context_send.at[k - 1], context_recv.at[k - 1],
+             along_depth(k))
+        for k in range(1, GROUP)
+    ]
+    for copy in context_copies:
+        copy.start()
+    row_buf[depth] = rows_ref[depth]
+    place_buf[depth] = place_ref[...]
+    weights[plane] = weight_ref[...]
+    contexts[depth] = context_ref[...]
+
+    for copy in place_copies:
+        copy.wait()
+    places = place_buf[0, 0:1, :]
+    for j in range(1, GROUP):
+        places = places + place_buf[j, 0:1, :]
+    source_rows = row_buf.shape[1]
+    width = row_buf.shape[2]
+    wanted = lax.broadcasted_iota(jnp.int32, (GROUP * block, GROUP * source_rows), 0)
+    choice = jnp.where(wanted == places, 1.0, 0.0).astype(jnp.bfloat16)
+    for copy in row_copies:
+        copy.wait()
+    routed[...] = (
+        jnp.dot(
+            choice, row_buf[...].reshape(GROUP * source_rows, width),
+            preferred_element_type=jnp.float32,
+        )
+        .astype(jnp.bfloat16)
+        .reshape(GROUP, block, width)
+    )
+    mine = core * GROUP + plane
+    routed_copies = []
+    for k in range(1, GROUP):
+        for which, owner in enumerate((core, other)):
+            index = 2 * (k - 1) + which
+            routed_copies.append(
+                send(routed.at[ahead(plane, k)], arrived.at[mine],
+                     routed_send.at[index], routed_recv.at[index], along_plane(k, owner))
+            )
+    routed_copies.append(
+        send(routed.at[plane], arrived.at[mine], routed_send.at[2 * (GROUP - 1)],
+             routed_recv.at[2 * (GROUP - 1)], (e, other))
+    )
+    for copy in routed_copies:
+        copy.start()
+    arrived[mine] = routed[plane]
+
+    total = GROUP * slots
+    slot = lax.broadcasted_iota(jnp.int32, (total, 1), 0)
+    fifth = (slot * (2**18 // capacity + 1)) >> 18
+    arrival = slot - fifth * capacity
+    plane_of, source_depth = fifth & 3, (fifth >> 2) & 3
+    core_of, target_depth = (fifth >> 4) & 1, fifth >> 5
+    found = (
+        (core_of * GROUP + plane_of) * block
+        + (target_depth * GROUP + source_depth) * capacity
+        + arrival
+    )
+    order = jnp.where(
+        lax.broadcasted_iota(jnp.int32, (total, total), 1) == found, 1.0, 0.0
+    ).astype(jnp.bfloat16)
+    for copy in routed_copies:
+        copy.wait()
+    ordered = jnp.dot(
+        order, arrived[...].reshape(total, width), preferred_element_type=jnp.float32
+    )
+    grads[...] = ordered.astype(jnp.bfloat16).reshape(GROUP, slots, width)
+    grads_t[...] = (
+        ordered.T[: GROUP * features, :].astype(jnp.bfloat16).reshape(GROUP, features, total)
+    )
+
+    for copy in weight_copies:
+        copy.wait()
+
+    def gc_copy(k):
+        return send(context_out.at[ahead(depth, k)], context_in.at[depth],
+                    gc_send.at[k - 1], gc_recv.at[k - 1], along_depth(k))
+
+    def context_step(k, carry):
+        at = ahead(depth, k)
+        context_out[at] = jnp.dot(
+            grads[at][:, : GROUP * features],
+            weights[...].reshape(GROUP * features, -1),
+            preferred_element_type=jnp.float32,
+        ).astype(jnp.bfloat16)
+
+        @pl.when(k < GROUP)
+        def _():
+            gc_copy(k).start()
+
+        return carry
+
+    lax.fori_loop(1, GROUP + 1, context_step, 0)
+
+    for copy in context_copies:
+        copy.wait()
+
+    def gw_copy(k):
+        return send(weight_out.at[ahead(plane, k)], weight_in.at[plane],
+                    gw_send.at[k - 1], gw_recv.at[k - 1], along_plane(k, core))
+
+    def weight_step(k, carry):
+        at = ahead(plane, k)
+        weight_out[at] = jnp.dot(
+            grads_t[at], contexts[...].reshape(total, -1), preferred_element_type=jnp.float32
+        ).astype(jnp.bfloat16)
+
+        @pl.when(k < GROUP)
+        def _():
+            gw_copy(k).start()
+
+        return carry
+
+    lax.fori_loop(1, GROUP + 1, weight_step, 0)
+
+    for k in range(1, GROUP):
+        gw_copy(k).wait()
+    summed = weight_out[plane].astype(jnp.float32)
+    for k in range(1, GROUP):
+        summed = summed + weight_in[ahead(plane, GROUP - k)].astype(jnp.float32)
+    real = grad_weight_ref.shape[0]
+    grad_weight_ref[...] = summed[:real, :] * rescale
+    product = summed * weight_ref[...].astype(jnp.float32)
+    lanes = product[:, :BLOCK]
+    for j in range(1, product.shape[1] // BLOCK):
+        lanes = lanes + product[:, j * BLOCK : (j + 1) * BLOCK]
+    own = jnp.sum(lanes.T, axis=0, keepdims=True) * rescale
+    pad = scale_pair.shape[2] - features
+    own = jnp.broadcast_to(jnp.pad(own, ((0, 0), (0, pad))), scale_pair.shape[1:])
+
+    scale_pair[0] = own
+    pair = send(scale_pair.at[0], scale_pair.at[1], pair_send.at[0], pair_recv.at[0], (e, other))
+    pair.start()
+    pair.wait()
+    scale_group[plane] = scale_pair[0] + scale_pair[1]
+    group_copies = [
+        send(scale_group.at[plane], scale_group.at[plane], group_send.at[k - 1],
+             group_recv.at[k - 1], along_plane(k, core))
+        for k in range(1, GROUP)
+    ]
+    for copy in group_copies:
+        copy.start()
+    for copy in group_copies:
+        copy.wait()
+    all_copies = [
+        send(scale_group, scale_ref.at[depth], all_send.at[k - 1], all_recv.at[k - 1],
+             along_depth(k))
+        for k in range(1, GROUP)
+    ]
+    for copy in all_copies:
+        copy.start()
+    scale_ref[depth] = scale_group[...]
+
+    for k in range(1, GROUP):
+        gc_copy(k).wait()
+    gathered = context_out[depth].astype(jnp.float32)
+    for k in range(1, GROUP):
+        gathered = gathered + context_in[ahead(depth, GROUP - k)].astype(jnp.float32)
+    grad_context_ref[...] = gathered.astype(jnp.bfloat16)
+    for copy in all_copies:
+        copy.wait()
+
+
+def two_level(grad_rows, row_target, stored_context, block_scale, w_out, layer_scale):
+    encoders = lax.axis_size("edata")
+    owners = lax.axis_size("llm")
+    source_rows, features = grad_rows.shape
+    slot_count, columns = stored_context.shape
+    capacity = slot_count // (encoders * owners)
+    depth = lax.axis_index("edata") // GROUP
+    share = features // encoders
+    padded = up(share, 16)
+    width = up(GROUP * padded, 128)
+    block = GROUP * GROUP * capacity
+
+    scaled = (grad_rows.astype(jnp.float32) * layer_scale[None, :]).astype(jnp.bfloat16)
+    rows = jnp.pad(
+        scaled.reshape(source_rows, encoders, share), ((0, 0), (0, 0), (0, padded - share))
+    ).reshape(source_rows, GROUP, GROUP * padded)
+    rows = jnp.pad(rows, ((0, 0), (0, 0), (0, width - GROUP * padded))).transpose(1, 0, 2)
+
+    targets = row_target[:, 0]
+    earlier = jnp.arange(source_rows)[None, :] < jnp.arange(source_rows)[:, None]
+    same = targets[None, :] == targets[:, None]
+    arrival = jnp.sum(jnp.where(earlier & same, 1, 0).astype(jnp.int32), axis=1)
+    place = (
+        (targets % GROUP) * block
+        + ((targets // GROUP) * GROUP + depth) * capacity
+        + arrival
+    )
+    lane = jnp.arange(GROUP * source_rows)
+    place = jnp.where(lane // source_rows == depth, jnp.tile(place, GROUP), 0)
+    place = jnp.broadcast_to(place[None, :], (8, GROUP * source_rows)).astype(jnp.int32)
+
+    stored = stored_context.astype(jnp.float32).reshape(slot_count, -1, BLOCK)
+    context = (stored * block_scale[:, :, None]).reshape(slot_count, -1).astype(jnp.bfloat16)
+    weight = jnp.pad(w_out.T, ((0, padded - share), (0, 0)))
+    rescale = 1.0 / math.sqrt(source_rows * encoders * owners)
+
+    total = GROUP * slot_count
+    bf16, f32 = jnp.bfloat16, jnp.float32
+    small = up(padded, 128)
+    sems = [3, 3, 3, 3, 3, 3, 3, 3, 7, 7, 3, 3, 3, 3, 1, 1, 3, 3, 3, 3]
+    grad_context, grad_weight, scales = pl.pallas_call(
+        functools.partial(kernel, capacity, rescale),
+        out_shape=(
+            jax.ShapeDtypeStruct((slot_count, columns), bf16),
+            jax.ShapeDtypeStruct((share, columns), f32),
+            jax.ShapeDtypeStruct((GROUP, GROUP, 8, small), f32),
+        ),
+        in_specs=[pl.BlockSpec(memory_space=pltpu.VMEM)] * 4,
+        out_specs=[pl.BlockSpec(memory_space=pltpu.VMEM)] * 3,
+        scratch_shapes=[
+            pltpu.VMEM((GROUP, source_rows, width), bf16),
+            pltpu.VMEM((GROUP, 8, GROUP * source_rows), jnp.int32),
+            pltpu.VMEM((GROUP, block, width), bf16),
+            pltpu.VMEM((owners * GROUP, block, width), bf16),
+            pltpu.VMEM((GROUP, slot_count, width), bf16),
+            pltpu.VMEM((GROUP, padded, total), bf16),
+            pltpu.VMEM((GROUP, slot_count, columns), bf16),
+            pltpu.VMEM((GROUP, padded, columns), bf16),
+            pltpu.VMEM((GROUP, slot_count, columns), bf16),
+            pltpu.VMEM((GROUP, slot_count, columns), bf16),
+            pltpu.VMEM((GROUP, padded, columns), bf16),
+            pltpu.VMEM((GROUP, padded, columns), bf16),
+            pltpu.VMEM((2, 8, small), f32),
+            pltpu.VMEM((GROUP, 8, small), f32),
+        ]
+        + [pltpu.SemaphoreType.DMA((n,)) for n in sems],
+        compiler_params=pltpu.CompilerParams(
+            collective_id=0, has_side_effects=True, vmem_limit_bytes=48 * 2**20
+        ),
+    )(rows, place, context, weight)
+    grad_scale = scales[:, :, 0, :share].reshape(features) / layer_scale
+    return (grad_context, grad_weight, grad_scale)
 
 
 def on_device(grad_rows, row_target, stored_context, block_scale, w_out, layer_scale):
@@ -57,6 +365,7 @@
         P(),
     )
     out_specs = (P("edata", "llm"), P("edata", "llm"), P())
+    two_levels = mesh.shape["edata"] == GROUP * GROUP and mesh.shape["llm"] == 2
     return jax.shard_map(
-        on_device, mesh=mesh, in_specs=in_specs, out_specs=out_specs, check_vma=False
-    )
+        two_level if two_levels else on_device, mesh=mesh, in_specs=in_specs, out_specs=out_specs, check_vma=False
+    )

time: 408 us -> 99.9 us (0.24)
  waiting for transfers between devices: 296 us -> 0 us
  Pallas kernels: 0 us -> 88.2 us
  blocking collectives: 60 us -> 0 us
  matrix products: 16.6 us -> 0 us
  between operations: 14.1 us -> 0.77 us
  starting transfers between devices: 8.39 us -> 0 us
  local copies, waits for them, and re-layouts: 4.12 us -> 8.45 us
    reduce_scatter x1 -> x0, waiting for transfers between devices: 206 us -> none  [on_device(): lax.psum_scatter(lax.dot_general(scaled, context, (((0,), (0,)), ((), ())...]
    pallas_call x0 -> x1, Pallas kernels: none -> 88.2 us  [two_level(): pl.pallas_call(functools.partial(kernel, capacity, rescale), out_shape=(j...]
    all_gather x1 -> x0, waiting for transfers between devices: 60.6 us -> none  [on_device(): weights = lax.all_gather(w_out, 'edata', axis=1, tiled=True)]
    psum x1 -> x0, blocking collectives: 57.4 us -> none  [on_device(): grad_scale = lax.psum(partial_scale, ('edata', 'llm')) * rescale]
    all_to_all x1 -> x0, waiting for transfers between devices: 28.2 us -> none  [on_device(): lax.all_to_all(outgoing, 'edata', split_axis=0, concat_axis=0, tiled=True)]
    dot_general x3 -> x0, matrix products: 16.6 us -> none  [the longest x1 6.59 us: on_device(): lax.dot_general(scaled, context, (((0,), (0,)), ((), ())), preferred_elem...]
    all_to_all x1 -> x0, starting transfers between devices: 8.31 us -> none  [on_device(): lax.all_to_all(outgoing, 'edata', split_axis=0, concat_axis=0, tiled=True)]
    unnamed x5 -> x13, local copies, waits for them, and re-layouts: 0.81 us -> 5.24 us
  transfers between devices with their start and end apart: 3 -> 0, of which waited for: 3 -> 0; matrix products, arithmetic and copies ran while one was open for 6% -> 0% of each run, Pallas kernels for 0% -> 0%
where the time goes in v1:
time: 99.9 us; the launch traced here: 99.5 us
  Pallas kernels  88.2 us (88%)
  local copies, waits for them, and re-layouts  8.45 us (8%)
  other arithmetic  2.06 us (2%)
    pallas_call x1, Pallas kernels, two_level(): pl.pallas_call(functools.partial(kernel, capacity, rescale), out_shape=(j...  88.2 us
    unnamed x13, local copies, waits for them, and re-layouts  5.24 us

profile of v1, /device:TPU:0, one launch (start us, length us, event | category | flops | bytes accessed | tf_op | source)
XLA Modules:
  0.0 99.5 jit_solution(10344303929247958313)
XLA Ops:
  0.6 0.0 copy-start.4
  0.7 0.6 copy-done.4
  1.3 0.2 select_reduce_fusion
  1.5 0.0 copy-start.3
  1.5 0.1 tile.10
  1.6 0.6 copy-done.3
  2.2 0.0 copy-start.2
  2.2 0.1 copy.13
  2.3 0.6 copy-done.2
  2.9 1.1 %multiply_convert_fusion = bf16[64,3200]{1,0:T(8,128)(2,1)S(1)} fusion(bf16[64,3200]{1,0:T(8,128)(2,1)} %param.6, f32[3200]{0:T(1024)S(1)} %copy-done.2), kind=kLoop, calls=%fused_computation | loop fusion | flops 614400 | bytes 832000 | tf_op jit(solution)/shard_map/convert_element_type | solution.py:257
  4.0 1.6 %reshape.93 = bf16[64,16,200]{2,1,0:T(8,128)(2,1)S(1)} reshape(bf16[64,3200]{1,0:T(8,128)(2,1)S(1)} %multiply_convert_fusion) | data formatting | bytes 819200 | tf_op jit(solution)/shard_map/reshape | solution.py:259
  5.6 0.1 pad.12
  5.7 0.9 reshape.94
  6.6 0.1 copy.12
  6.7 0.0 copy-start
  6.7 0.9 copy-done
  7.7 0.0 copy-start.1
  7.7 0.2 mul.54
  8.0 0.7 copy-done.1
  8.7 0.2 fusion.context_ref
  8.9 88.2 %shard_map.85 = (bf16[160,1024]{1,0:T(8,128)(2,1)S(1)}, f32[200,1024]{1,0:T(8,128)S(1)}, f32[4,4,8,256]{3,2,1,0:T(8,128)S(1)}) custom-call(bf16[4,64,896]{2,1,0:T(8,128)(2,1)S(1)} %pad_bitcast_fusion.rows_ref, s32[8,256]{1,0:T(8,128)S(1)} %broadcast_in_dim.22.place_ref, bf16[160,1024]{1,0:T(8,128)(2,1)S(1)} %fusion.context_ref, ...), custom_call_target="tpu_custom_call" | custom-call | tf_op jit(solution)/shard_map/pallas_call | solution.py:285
  97.1 0.1 slice_reduce_fusion
  97.2 0.1 reshape_squeeze.3
  97.3 0.6 div.40
  97.9 0.7 copy.18
  98.6 0.9 copy.19
  (6 shorter events, 0.1 us)
Async XLA Ops:
  0.6 0.7 copy-start.4
  1.5 0.7 copy-start.3
  2.2 0.7 copy-start.2
  6.7 1.0 %copy-start = (bf16[1024,200]{0,1:T(8,128)(2,1)S(1)}, bf16[1024,200]{0,1:T(8,128)(2,1)}, u32[]{:S(2)}) copy-start(bf16[1024,200]{0,1:T(8,128)(2,1)} %param.10) | copy-start | bytes 1228804
  7.7 1.0 copy-start.1

commit v2 on v1

v2 whole, which is shorter than its diff:
```python
import functools
import math

import jax
import jax.numpy as jnp
from jax import lax
from jax.experimental import pallas as pl
from jax.experimental.pallas import tpu as pltpu
from jax.sharding import PartitionSpec as P

BLOCK = 128
GROUP = 4
MESH = pl.DeviceIdType.MESH


def up(value, unit):
    return -(-value // unit) * unit


def kernel(
    capacity, rescale, gradient_ref, target_ref, stored_ref, block_ref, weight_in_ref, layer_ref,
    grad_context_ref, grad_weight_ref, scale_ref,
    gradient, scaled, stored, row_buf, place_buf, routed, arrived, grads, grads_t, contexts,
    weights, context_own, up_out, up_in, down_out, down_in, weight_out, weight_in,
    scale_plane, scale_group,
    load_sem, row_send, row_recv, place_send, place_recv, weight_send, weight_recv,
    routed_send, routed_recv, cu_send, cu_recv, cd_send, cd_recv, gu_send, gu_recv,
    gd_send, gd_recv, gw_send, gw_recv, plane_send, plane_recv, all_send, all_recv,
):
    e, core = lax.axis_index("edata"), lax.axis_index("llm")
    depth, plane = e // GROUP, e % GROUP
    other = 1 - core
    last = GROUP - 1
    share = weight_in_ref.shape[0]
    features = weights.shape[1]
    slots = stored.shape[0]
    block = routed.shape[1]
    source_rows, width = row_buf.shape[1:]

    def ahead(own, k):
        return (own + k) % GROUP

    def along_depth(k):
        return (ahead(depth, k) * GROUP + plane, core)

    def along_plane(k, owner):
        return (depth * GROUP + ahead(plane, k), owner)

    def send(src, dst, send_sem, recv_sem, device):
        return pltpu.make_async_remote_copy(
            src_ref=src, dst_ref=dst, send_sem=send_sem, recv_sem=recv_sem,
            device_id=device, device_id_type=MESH,
        )

    loads = [
        pltpu.make_async_copy(gradient_ref, gradient, load_sem.at[0]),
        pltpu.make_async_copy(stored_ref, stored, load_sem.at[1]),
    ]
    for copy in loads:
        copy.start()
    barrier = pltpu.get_barrier_semaphore()
    for k in range(1, GROUP):
        pl.semaphore_signal(barrier, inc=1, device_id=along_depth(k), device_id_type=MESH)
        for owner in (core, other):
            pl.semaphore_signal(
                barrier, inc=1, device_id=along_plane(k, owner), device_id_type=MESH
            )
    pl.semaphore_signal(barrier, inc=1, device_id=(e, other), device_id_type=MESH)

    target = jnp.broadcast_to(target_ref[...], (source_rows, source_rows))
    first = lax.broadcasted_iota(jnp.int32, (source_rows, source_rows), 0)
    second = lax.broadcasted_iota(jnp.int32, (source_rows, source_rows), 1)
    column = target.astype(jnp.float32).T.astype(jnp.int32)
    before = jnp.where((target == column) & (first < second), 1.0, 0.0)
    arrival = jnp.sum(before, axis=0, keepdims=True).astype(jnp.int32)
    target = target_ref[...]
    place = (target & 3) * block + ((target >> 2) * GROUP + depth) * capacity + arrival
    spread = jnp.concatenate([place] * GROUP, axis=1)
    lane = lax.broadcasted_iota(jnp.int32, spread.shape, 1)
    begin = depth * source_rows
    inside = (lane >= begin) & (lane < begin + source_rows)
    place_buf[depth] = jnp.broadcast_to(jnp.where(inside, spread, 0), place_buf.shape[1:])
    weights[plane, :share, :] = weight_in_ref[...]
    weights[plane, share:, :] = jnp.zeros((features - share, weights.shape[2]), weights.dtype)
    loads[0].wait()
    scaled[...] = (gradient[...].astype(jnp.float32) * layer_ref[...]).astype(jnp.bfloat16)
    pl.semaphore_wait(barrier, 3 * last + 1)

    def window(at):
        return pl.multiple_of((at * (GROUP * share)) // BLOCK * BLOCK, BLOCK)

    row_copies = []
    place_copies = []
    for k in range(1, GROUP):
        row_copies.append(
            send(scaled.at[:, pl.ds(window(ahead(depth, k)), width)], row_buf.at[depth],
                 row_send.at[k - 1], row_recv.at[k - 1], along_depth(k))
        )
        place_copies.append(
            send(place_buf.at[depth], place_buf.at[depth],
                 place_send.at[k - 1], place_recv.at[k - 1], along_depth(k))
        )
    for copy in place_copies + row_copies:
        copy.start()
    weight_copies = [
        send(weights.at[plane], weights.at[plane], weight_send.at[k - 1], weight_recv.at[k - 1],
             along_plane(k, core))
        for k in range(1, GROUP)
    ]
    for copy in weight_copies:
        copy.start()
    row_buf[depth] = scaled[:, pl.ds(window(depth), width)]

    loads[1].wait()
    factors = block_ref[...].T
    for j in range(factors.shape[1]):
        part = slice(j * BLOCK, (j + 1) * BLOCK)
        contexts[depth, :, part] = (
            stored[:, part].astype(jnp.float32) * factors[:, j : j + 1]
        ).astype(jnp.bfloat16)

    def context_up(s):
        return send(contexts.at[depth - s], contexts.at[depth - s], cu_send.at[s],
                    cu_recv.at[s], ((depth + 1) * GROUP + plane, core))

    def context_down(s):
        return send(contexts.at[depth + s], contexts.at[depth + s], cd_send.at[s],
                    cd_recv.at[s], ((depth - 1) * GROUP + plane, core))

    def context_wait(s):
        @pl.when(depth - 1 - s >= 0)
        def _():
            below = contexts.at[depth - 1 - s]
            send(below, below, cu_send.at[s], cu_recv.at[s], (e, other)).wait_recv()

        @pl.when(depth + 1 + s <= last)
        def _():
            above = contexts.at[depth + 1 + s]
            send(above, above, cd_send.at[s], cd_recv.at[s], (e, other)).wait_recv()

    def context_step(s):
        if s > 0:
            context_wait(s - 1)

        @pl.when((depth < last) & (depth - s >= 0))
        def _():
            context_up(s).start()

        @pl.when((depth > 0) & (depth + s <= last))
        def _():
            context_down(s).start()

    lane = lax.broadcasted_iota(jnp.int32, (1, GROUP * features), 1)
    part = jnp.zeros_like(lane)
    for k in range(1, GROUP):
        part = part + jnp.where(lane >= k * features, 1, 0)
    within = lane - part * features
    source = depth * (GROUP * share) - window(depth) + part * share + within
    source = jnp.where(within < share, source, -1)
    select = jnp.where(
        lax.broadcasted_iota(jnp.int32, (width, GROUP * features), 0) == source, 1.0, 0.0
    ).astype(jnp.bfloat16)

    for copy in place_copies:
        copy.wait()
    places = place_buf[0, 0:1, :]
    for j in range(1, GROUP):
        places = places + place_buf[j, 0:1, :]
    wanted = lax.broadcasted_iota(jnp.int32, (GROUP * block, GROUP * source_rows), 0)
    choice = jnp.where(wanted == places, 1.0, 0.0).astype(jnp.bfloat16)
    for copy in row_copies:
        copy.wait()
    context_step(0)
    owned = jnp.dot(
        row_buf[...].reshape(GROUP * source_rows, width), select,
        preferred_element_type=jnp.float32,
    ).astype(jnp.bfloat16)
    routed[...] = (
        jnp.dot(choice, owned, preferred_element_type=jnp.float32)
        .astype(jnp.bfloat16)
        .reshape(GROUP, block, GROUP * features)
    )
    mine = core * GROUP + plane
    routed_copies = []
    for k in range(1, GROUP):
        for which, owner in enumerate((core, other)):
            index = 2 * (k - 1) + which
            routed_copies.append(
                send(routed.at[ahead(plane, k)], arrived.at[mine],
                     routed_send.at[index], routed_recv.at[index], along_plane(k, owner))
            )
    routed_copies.append(
        send(routed.at[plane], arrived.at[mine], routed_send.at[2 * last],
             routed_recv.at[2 * last], (e, other))
    )
    for copy in routed_copies:
        copy.start()
    arrived[mine] = routed[plane]
    context_step(1)

    total = GROUP * slots
    slot = lax.broadcasted_iota(jnp.int32, (total, 1), 0)
    fifth = (slot * (2**18 // capacity + 1)) >> 18
    found_arrival = slot - fifth * capacity
    plane_of, source_depth = fifth & 3, (fifth >> 2) & 3
    core_of, target_depth = (fifth >> 4) & 1, fifth >> 5
    found = (
        (core_of * GROUP + plane_of) * block
        + (target_depth * GROUP + source_depth) * capacity
        + found_arrival
    )
    order = jnp.where(
        lax.broadcasted_iota(jnp.int32, (total, total), 1) == found, 1.0, 0.0
    ).astype(jnp.bfloat16)
    context_step(2)
    for copy in routed_copies:
        copy.wait()
    ordered = jnp.dot(
        order, arrived[...].reshape(total, GROUP * features), preferred_element_type=jnp.float32
    )
    grads[...] = ordered.astype(jnp.bfloat16).reshape(GROUP, slots, GROUP * features)
    grads_t[...] = ordered.T.astype(jnp.bfloat16).reshape(GROUP, features, total)

    for copy in weight_copies:
        copy.wait()

    def own_step(k, carry):
        at = (depth + 2 + k) % GROUP
        context_own[at] = jnp.dot(
            grads[at], weights[...].reshape(GROUP * features, -1),
            preferred_element_type=jnp.float32,
        )
        return carry

    lax.fori_loop(0, GROUP, own_step, 0)

    def sum_up(s):
        return send(up_out.at[s], up_in.at[s], gu_send.at[s], gu_recv.at[s],
                    ((depth + 1) * GROUP + plane, core))

    def sum_down(s):
        return send(down_out.at[s], down_in.at[s], gd_send.at[s], gd_recv.at[s],
                    ((depth - 1) * GROUP + plane, core))

    def up_wait(s):
        send(up_in.at[s], up_in.at[s], gu_send.at[s], gu_recv.at[s], (e, other)).wait_recv()

    def down_wait(s):
        send(down_in.at[s], down_in.at[s], gd_send.at[s], gd_recv.at[s], (e, other)).wait_recv()

    def sum_step(s):
        @pl.when((depth < last) & (depth <= s))
        def _():
            at = last + depth - s
            if s == 0:
                up_out[s] = context_own[at].astype(jnp.bfloat16)
            else:

                @pl.when(depth == 0)
                def _():
                    up_out[s] = context_own[at].astype(jnp.bfloat16)

                @pl.when(depth > 0)
                def _():
                    up_wait(s - 1)
                    up_out[s] = (
                        context_own[at] + up_in[s - 1].astype(jnp.float32)
                    ).astype(jnp.bfloat16)

            sum_up(s).start()

        @pl.when((depth > 0) & (last - depth <= s))
        def _():
            at = depth - last + s
            if s == 0:
                down_out[s] = context_own[at].astype(jnp.bfloat16)
            else:

                @pl.when(depth == last)
                def _():
                    down_out[s] = context_own[at].astype(jnp.bfloat16)

                @pl.when(depth < last)
                def _():
                    down_wait(s - 1)
                    down_out[s] = (
                        context_own[at] + down_in[s - 1].astype(jnp.float32)
                    ).astype(jnp.bfloat16)

            sum_down(s).start()

    sum_step(0)

    context_wait(2)

    def gw_copy(k):
        return send(weight_out.at[ahead(plane, k)], weight_in.at[plane],
                    gw_send.at[k - 1], gw_recv.at[k - 1], along_plane(k, core))

    def weight_step(k, carry):
        at = ahead(plane, k)
        weight_out[at] = jnp.dot(
            grads_t[at], contexts[...].reshape(total, -1), preferred_element_type=jnp.float32
        ).astype(jnp.bfloat16)

        @pl.when(k < GROUP)
        def _():
            gw_copy(k).start()

        return carry

    lax.fori_loop(1, GROUP + 1, weight_step, 0)
    sum_step(1)
    sum_step(2)

    for k in range(1, GROUP):
        gw_copy(k).wait()
    summed = weight_out[plane].astype(jnp.float32)
    for k in range(1, GROUP):
        summed = summed + weight_in[ahead(plane, GROUP - k)].astype(jnp.float32)
    product = summed * weights[plane].astype(jnp.float32)
    lanes = product[:, :BLOCK]
    for j in range(1, product.shape[1] // BLOCK):
        lanes = lanes + product[:, j * BLOCK : (j + 1) * BLOCK]
    own = jnp.sum(lanes.T, axis=0, keepdims=True) * rescale
    pad = scale_plane.shape[2] - features
    own = jnp.broadcast_to(jnp.pad(own, ((0, 0), (0, pad))), scale_plane.shape[1:])

    scale_plane[mine] = own
    plane_copies = []
    for k in range(GROUP):
        for which, owner in enumerate((other, core)):
            if k > 0 or which == 0:
                index = 2 * k + which - (1 if k > 0 else 0)
                plane_copies.append(
                    send(scale_plane.at[mine], scale_plane.at[mine], plane_send.at[index],
                         plane_recv.at[index], along_plane(k, owner))
                )
    for copy in plane_copies:
        copy.start()
    grad_weight_ref[...] = summed[:share, :] * rescale
    for copy in plane_copies:
        copy.wait()
    for j in range(GROUP):
        scale_group[j] = scale_plane[j] + scale_plane[GROUP + j]
    all_copies = [
        send(scale_group, scale_ref.at[depth], all_send.at[k - 1], all_recv.at[k - 1],
             along_depth(k))
        for k in range(1, GROUP)
    ]
    for copy in all_copies:
        copy.start()
    scale_ref[depth] = scale_group[...]

    @pl.when(depth > 0)
    def _():
        up_wait(2)
        context_own[depth] += up_in[2].astype(jnp.float32)

    @pl.when(depth < last)
    def _():
        down_wait(2)
        context_own[depth] += down_in[2].astype(jnp.float32)

    grad_context_ref[...] = context_own[depth].astype(jnp.bfloat16)

    for s in range(last):

        @pl.when((depth < last) & (depth - s >= 0))
        def _():
            context_up(s).wait_send()

        @pl.when((depth > 0) & (depth + s <= last))
        def _():
            context_down(s).wait_send()

        @pl.when((depth < last) & (depth <= s))
        def _():
            sum_up(s).wait_send()

        @pl.when((depth > 0) & (last - depth <= s))
        def _():
            sum_down(s).wait_send()

    for copy in all_copies:
        copy.wait()


def two_level(grad_rows, row_target, stored_context, block_scale, w_out, layer_scale):
    encoders = lax.axis_size("edata")
    owners = lax.axis_size("llm")
    source_rows, features = grad_rows.shape
    slot_count, columns = stored_context.shape
    capacity = slot_count // (encoders * owners)
    share = features // encoders
    padded = up(share, 16)
    starts = [d * GROUP * share // BLOCK * BLOCK for d in range(GROUP)]
    width = max(up((d + 1) * GROUP * share, BLOCK) - starts[d] for d in range(GROUP))
    block = GROUP * GROUP * capacity
    rescale = 1.0 / math.sqrt(source_rows * encoders * owners)

    total = GROUP * slot_count
    bf16, f32 = jnp.bfloat16, jnp.float32
    small = up(padded, 128)
    sems = [2, 3, 3, 3, 3, 3, 3, 7, 7, 3, 3, 3, 3, 3, 3, 3, 3, 3, 3, 7, 7, 3, 3]
    vmem = pl.BlockSpec(memory_space=pltpu.VMEM)
    far = pl.BlockSpec(memory_space=pl.ANY)
    grad_context, grad_weight, scales = pl.pallas_call(
        functools.partial(kernel, capacity, rescale),
        out_shape=(
            jax.ShapeDtypeStruct((slot_count, columns), bf16),
            jax.ShapeDtypeStruct((share, columns), f32),
            jax.ShapeDtypeStruct((GROUP, GROUP, 8, small), f32),
        ),
        in_specs=[far, vmem, far, vmem, vmem, vmem],
        out_specs=[vmem] * 3,
        scratch_shapes=[
            pltpu.VMEM((source_rows, features), bf16),
            pltpu.VMEM((source_rows, features), bf16),
            pltpu.VMEM((slot_count, columns), bf16),
            pltpu.VMEM((GROUP, source_rows, width), bf16),
            pltpu.VMEM((GROUP, 8, GROUP * source_rows), jnp.int32),
            pltpu.VMEM((GROUP, block, GROUP * padded), bf16),
            pltpu.VMEM((owners * GROUP, block, GROUP * padded), bf16),
            pltpu.VMEM((GROUP, slot_count, GROUP * padded), bf16),
            pltpu.VMEM((GROUP, padded, total), bf16),
            pltpu.VMEM((GROUP, slot_count, columns), bf16),
            pltpu.VMEM((GROUP, padded, columns), bf16),
            pltpu.VMEM((GROUP, slot_count, columns), f32),
            pltpu.VMEM((GROUP - 1, slot_count, columns), bf16),
            pltpu.VMEM((GROUP - 1, slot_count, columns), bf16),
            pltpu.VMEM((GROUP - 1, slot_count, columns), bf16),
            pltpu.VMEM((GROUP - 1, slot_count, columns), bf16),
            pltpu.VMEM((GROUP, padded, columns), bf16),
            pltpu.VMEM((GROUP, padded, columns), bf16),
            pltpu.VMEM((owners * GROUP, 8, small), f32),
            pltpu.VMEM((GROUP, 8, small), f32),
        ]
        + [pltpu.SemaphoreType.DMA((n,)) for n in sems],
        compiler_params=pltpu.CompilerParams(
            collective_id=0, has_side_effects=True, vmem_limit_bytes=48 * 2**20
        ),
    )(grad_rows, row_target.T, stored_context, block_scale.T, w_out.T, layer_scale[None, :])
    grad_scale = scales[:, :, 0, :share].reshape(features) / layer_scale
    return (grad_context, grad_weight, grad_scale)


def on_device(grad_rows, row_target, stored_context, block_scale, w_out, layer_scale):
    encoders = lax.axis_size("edata")
    owners = lax.axis_size("llm")
    source_rows = grad_rows.shape[0]
    features = grad_rows.shape[1]
    slot_count = stored_context.shape[0]
    capacity = slot_count // (encoders * owners)
    weights = lax.all_gather(w_out, "edata", axis=1, tiled=True)
    targets = row_target[:, 0]
    chosen = (targets[:, None] == jnp.arange(encoders, dtype=jnp.int32)[None, :]).astype(jnp.int32)
    arrival = jnp.sum(chosen * (jnp.cumsum(chosen, axis=0) - 1), axis=1)
    position = targets * capacity + arrival
    outgoing = jnp.zeros((encoders * capacity, features), jnp.bfloat16).at[position].set(grad_rows)
    arrived = lax.all_to_all(outgoing, "edata", split_axis=0, concat_axis=0, tiled=True)
    grad_slots = lax.all_gather(arrived, "llm", axis=0, tiled=True)
    stored = stored_context.astype(jnp.float32).reshape(slot_count, -1, BLOCK)
    context = (stored * block_scale[:, :, None]).reshape(slot_count, -1).astype(jnp.bfloat16)
    scaled = (grad_slots.astype(jnp.float32) * layer_scale[None, :]).astype(jnp.bfloat16)
    recomputed = jnp.dot(context, weights, preferred_element_type=jnp.float32)
    grad_context = lax.dot_general(
        scaled, weights, (((1,), (1,)), ((), ())), preferred_element_type=jnp.float32
    ).astype(jnp.bfloat16)
    partial_scale = jnp.sum(grad_slots.astype(jnp.float32) * recomputed, axis=0)
    rescale = 1.0 / math.sqrt(source_rows * encoders * owners)
    grad_weight = (
        lax.psum_scatter(
            lax.dot_general(
                scaled, context, (((0,), (0,)), ((), ())), preferred_element_type=jnp.float32
            ),
            "edata",
            scatter_dimension=0,
            tiled=True,
        )
        * rescale
    )
    grad_scale = lax.psum(partial_scale, ("edata", "llm")) * rescale
    return (grad_context, grad_weight, grad_scale)


def solution(mesh):
    in_specs = (
        P(("edata", "llm"), None),
        P(("edata", "llm"), None),
        P("edata", "llm"),
        P("edata", "llm"),
        P("llm", "edata"),
        P(),
    )
    out_specs = (P("edata", "llm"), P("edata", "llm"), P())
    two_levels = mesh.shape["edata"] == GROUP * GROUP and mesh.shape["llm"] == 2
    return jax.shard_map(
        two_level if two_levels else on_device, mesh=mesh, in_specs=in_specs, out_specs=out_specs, check_vma=False
    )
```

time: 99.9 us -> 79.2 us (0.79)
  Pallas kernels: 88.2 us -> 71.4 us
  local copies, waits for them, and re-layouts: 8.45 us -> 6.09 us
  other arithmetic: 2.06 us -> 0.61 us
    pallas_call x1, Pallas kernels: 88.2 us -> 71.4 us  [two_level(): pl.pallas_call(functools.partial(kernel, capacity, rescale), out_shape=(j...]
    reshape x3 -> x0, local copies, waits for them, and re-layouts: 2.57 us -> none  [the longest x1 1.57 us: two_level(): scaled.reshape(source_rows, encoders, share)]
    convert_element_type x2 -> x0, other arithmetic: 1.25 us -> none  [the longest x1 1.07 us: two_level(): (grad_rows.astype(jnp.float32) * layer_scale[None, :]).astype(jnp.bfloat16)]
    unnamed x13 -> x14, local copies, waits for them, and re-layouts: 5.24 us -> 5.19 us
where the time goes in v2:
time: 79.2 us; the launch traced here: 78.8 us
  Pallas kernels  71.4 us (90%)
  local copies, waits for them, and re-layouts  6.09 us (8%)
    pallas_call x1, Pallas kernels, two_level(): pl.pallas_call(functools.partial(kernel, capacity, rescale), out_shape=(j...  71.4 us
    unnamed x14, local copies, waits for them, and re-layouts  5.19 us

profile of v2, /device:TPU:0, one launch (start us, length us, event | category | flops | bytes accessed | tf_op | source)
XLA Modules:
  0.0 78.8 jit_solution(4380977024375309425)
XLA Ops:
  0.6 0.0 copy-start.3
  0.6 0.0 copy-start.4
  0.7 0.7 broadcast_in_dim.3.layer_ref
  1.4 0.0 copy-done.3
  1.4 0.0 copy-done.4
  1.4 0.0 copy-start
  1.4 1.0 %copy-done = bf16[64,3200]{1,0:T(8,128)(2,1)S(1)} copy-done((bf16[64,3200]{1,0:T(8,128)(2,1)S(1)}, bf16[64,3200]{1,0:T(8,128)(2,1)}, u32[]{:S(2)}) %copy-start) | copy-done | bytes 409624
  2.4 0.0 copy-start.1
  2.4 1.0 %copy-done.1 = bf16[1024,200]{0,1:T(8,128)(2,1)S(1)} copy-done((bf16[1024,200]{0,1:T(8,128)(2,1)S(1)}, bf16[1024,200]{0,1:T(8,128)(2,1)}, u32[]{:S(2)}) %copy-start.1) | copy-done | bytes 409624
  3.4 0.0 copy-start.2
  3.4 1.0 %copy-done.2 = bf16[160,1024]{1,0:T(8,128)(2,1)S(1)} copy-done((bf16[160,1024]{1,0:T(8,128)(2,1)S(1)}, bf16[160,1024]{1,0:T(8,128)(2,1)}, u32[]{:S(2)}) %copy-start.2) | copy-done | bytes 327704
  4.4 71.4 %shard_map.85 = (bf16[160,1024]{1,0:T(8,128)(2,1)S(1)}, f32[200,1024]{1,0:T(8,128)S(1)}, f32[4,4,8,256]{3,2,1,0:T(8,128)S(1)}) custom-call(bf16[64,3200]{1,0:T(8,128)(2,1)S(1)} %copy-done, s32[1,64]{1,0:T(1,128)S(1)} %bitcast.5, bf16[160,1024]{1,0:T(8,128)(2,1)S(1)} %copy-done.2, f32[8,160]{1,0:T(8,128)S(1)} %bitcast.4, bf16[200,1024]{1,0:T(8,128)(2,1)S(1)} %bitcast.3, ...), custom_call_target="tpu_custom_call" | custom-call | tf_op jit(solution)/shard_map/pallas_call | solution.py:408
  75.8 0.1 slice_reduce_fusion
  75.9 0.0 copy-start.5
  75.9 0.1 reshape_squeeze.3
  76.0 0.6 copy-done.5
  76.6 0.6 div.3
  77.2 0.7 copy.11
  78.0 0.9 %copy.12 = f32[200,1024]{1,0:T(8,128)} copy(f32[200,1024]{1,0:T(8,128)S(1)} %get-tuple-element.13) | data formatting | bytes 1638400
Async XLA Ops:
  0.6 0.8 copy-start.3
  0.6 0.8 copy-start.4
  1.4 1.0 %copy-start = (bf16[64,3200]{1,0:T(8,128)(2,1)S(1)}, bf16[64,3200]{1,0:T(8,128)(2,1)}, u32[]{:S(2)}) copy-start(bf16[64,3200]{1,0:T(8,128)(2,1)} %gradient_ref.1) | copy-start | bytes 1228804
  2.4 1.0 %copy-start.1 = (bf16[1024,200]{0,1:T(8,128)(2,1)S(1)}, bf16[1024,200]{0,1:T(8,128)(2,1)}, u32[]{:S(2)}) copy-start(bf16[1024,200]{0,1:T(8,128)(2,1)} %param.10) | copy-start | bytes 1228804
  3.4 1.0 %copy-start.2 = (bf16[160,1024]{1,0:T(8,128)(2,1)S(1)}, bf16[160,1024]{1,0:T(8,128)(2,1)}, u32[]{:S(2)}) copy-start(bf16[160,1024]{1,0:T(8,128)(2,1)} %stored_ref.1) | copy-start | bytes 983044
  75.9 0.7 copy-start.5

commit v3 on v2

--- a/solution.py
+++ b/solution.py
@@ -18,9 +18,9 @@
 
 
 def kernel(
-    capacity, rescale, gradient_ref, target_ref, stored_ref, block_ref, weight_in_ref, layer_ref,
+    capacity, rescale, gradient_ref, target_ref, stored_ref, block_ref, weight_in_ref, layer_in_ref,
     grad_context_ref, grad_weight_ref, scale_ref,
-    gradient, scaled, stored, row_buf, place_buf, routed, arrived, grads, grads_t, contexts,
+    gradient, scaled, stored, targets, blocks, weight_own, layer, row_buf, place_buf, routed, arrived, grads, grads_t, contexts,
     weights, context_own, up_out, up_in, down_out, down_in, weight_out, weight_in,
     scale_plane, scale_group,
     load_sem, row_send, row_recv, place_send, place_recv, weight_send, weight_recv,
@@ -31,7 +31,7 @@
     depth, plane = e // GROUP, e % GROUP
     other = 1 - core
     last = GROUP - 1
-    share = weight_in_ref.shape[0]
+    share = weight_own.shape[0]
     features = weights.shape[1]
     slots = stored.shape[0]
     block = routed.shape[1]
@@ -54,7 +54,11 @@
 
     loads = [
         pltpu.make_async_copy(gradient_ref, gradient, load_sem.at[0]),
-        pltpu.make_async_copy(stored_ref, stored, load_sem.at[1]),
+        pltpu.make_async_copy(layer_in_ref, layer, load_sem.at[1]),
+        pltpu.make_async_copy(target_ref, targets, load_sem.at[2]),
+        pltpu.make_async_copy(weight_in_ref, weight_own, load_sem.at[3]),
+        pltpu.make_async_copy(stored_ref, stored, load_sem.at[4]),
+        pltpu.make_async_copy(block_ref, blocks, load_sem.at[5]),
     ]
     for copy in loads:
         copy.start()
@@ -67,23 +71,26 @@
             )
     pl.semaphore_signal(barrier, inc=1, device_id=(e, other), device_id_type=MESH)
 
-    target = jnp.broadcast_to(target_ref[...], (source_rows, source_rows))
+    loads[2].wait()
+    target = jnp.broadcast_to(targets[...], (source_rows, source_rows))
     first = lax.broadcasted_iota(jnp.int32, (source_rows, source_rows), 0)
     second = lax.broadcasted_iota(jnp.int32, (source_rows, source_rows), 1)
     column = target.astype(jnp.float32).T.astype(jnp.int32)
     before = jnp.where((target == column) & (first < second), 1.0, 0.0)
     arrival = jnp.sum(before, axis=0, keepdims=True).astype(jnp.int32)
-    target = target_ref[...]
+    target = targets[...]
     place = (target & 3) * block + ((target >> 2) * GROUP + depth) * capacity + arrival
     spread = jnp.concatenate([place] * GROUP, axis=1)
     lane = lax.broadcasted_iota(jnp.int32, spread.shape, 1)
     begin = depth * source_rows
     inside = (lane >= begin) & (lane < begin + source_rows)
     place_buf[depth] = jnp.broadcast_to(jnp.where(inside, spread, 0), place_buf.shape[1:])
-    weights[plane, :share, :] = weight_in_ref[...]
+    loads[3].wait()
+    weights[plane, :share, :] = weight_own[...]
     weights[plane, share:, :] = jnp.zeros((features - share, weights.shape[2]), weights.dtype)
     loads[0].wait()
-    scaled[...] = (gradient[...].astype(jnp.float32) * layer_ref[...]).astype(jnp.bfloat16)
+    loads[1].wait()
+    scaled[...] = (gradient[...].astype(jnp.float32) * layer[...].reshape(1, -1)).astype(jnp.bfloat16)
     pl.semaphore_wait(barrier, 3 * last + 1)
 
     def window(at):
@@ -102,17 +109,28 @@
         )
     for copy in place_copies + row_copies:
         copy.start()
+    half = weights.shape[2] // 2
+    beside = plane // 2 * 2 + (1 - plane % 2)
+    across = (1 - plane // 2) * 2 + plane % 2
+
+    def weight_copy(index, owner, part, to):
+        ref = weights.at[owner, :, pl.ds(part * half, half)]
+        return send(ref, ref, weight_send.at[index], weight_recv.at[index],
+                    (depth * GROUP + to, core))
+
     weight_copies = [
-        send(weights.at[plane], weights.at[plane], weight_send.at[k - 1], weight_recv.at[k - 1],
-             along_plane(k, core))
-        for k in range(1, GROUP)
+        weight_copy(0, plane, 0, beside),
+        weight_copy(1, plane, 1, across),
+        weight_copy(2, plane, 1, beside),
+        weight_copy(3, plane, 0, across),
     ]
     for copy in weight_copies:
         copy.start()
     row_buf[depth] = scaled[:, pl.ds(window(depth), width)]
 
-    loads[1].wait()
-    factors = block_ref[...].T
+    loads[4].wait()
+    loads[5].wait()
+    factors = blocks[...].T
     for j in range(factors.shape[1]):
         part = slice(j * BLOCK, (j + 1) * BLOCK)
         contexts[depth, :, part] = (
@@ -149,6 +167,8 @@
         @pl.when((depth > 0) & (depth + s <= last))
         def _():
             context_down(s).start()
+
+    context_step(0)
 
     lane = lax.broadcasted_iota(jnp.int32, (1, GROUP * features), 1)
     part = jnp.zeros_like(lane)
@@ -161,6 +181,20 @@
         lax.broadcasted_iota(jnp.int32, (width, GROUP * features), 0) == source, 1.0, 0.0
     ).astype(jnp.bfloat16)
 
+    total = GROUP * slots
+    slot = lax.broadcasted_iota(jnp.int32, (total, 1), 0)
+    fifth = (slot * (2**18 // capacity + 1)) >> 18
+    found_arrival = slot - fifth * capacity
+    plane_of, source_depth = fifth & 3, (fifth >> 2) & 3
+    core_of, target_depth = (fifth >> 4) & 1, fifth >> 5
+    found = (
+        (core_of * GROUP + plane_of) * block
+        + (target_depth * GROUP + source_depth) * capacity
+        + found_arrival
+    )
+    order = jnp.where(
+        lax.broadcasted_iota(jnp.int32, (total, total), 1) == found, 1.0, 0.0
+    ).astype(jnp.bfloat16)
     for copy in place_copies:
         copy.wait()
     places = place_buf[0, 0:1, :]
@@ -170,7 +204,6 @@
     choice = jnp.where(wanted == places, 1.0, 0.0).astype(jnp.bfloat16)
     for copy in row_copies:
         copy.wait()
-    context_step(0)
     owned = jnp.dot(
         row_buf[...].reshape(GROUP * source_rows, width), select,
         preferred_element_type=jnp.float32,
@@ -196,22 +229,12 @@
     for copy in routed_copies:
         copy.start()
     arrived[mine] = routed[plane]
+    weight_copies[0].wait_recv()
+    weight_copies[1].wait_recv()
+    passed = [weight_copy(4, beside, 0, across), weight_copy(5, across, 1, beside)]
+    for copy in passed:
+        copy.start()
     context_step(1)
-
-    total = GROUP * slots
-    slot = lax.broadcasted_iota(jnp.int32, (total, 1), 0)
-    fifth = (slot * (2**18 // capacity + 1)) >> 18
-    found_arrival = slot - fifth * capacity
-    plane_of, source_depth = fifth & 3, (fifth >> 2) & 3
-    core_of, target_depth = (fifth >> 4) & 1, fifth >> 5
-    found = (
-        (core_of * GROUP + plane_of) * block
-        + (target_depth * GROUP + source_depth) * capacity
-        + found_arrival
-    )
-    order = jnp.where(
-        lax.broadcasted_iota(jnp.int32, (total, total), 1) == found, 1.0, 0.0
-    ).astype(jnp.bfloat16)
     context_step(2)
     for copy in routed_copies:
         copy.wait()
@@ -221,75 +244,86 @@
     grads[...] = ordered.astype(jnp.bfloat16).reshape(GROUP, slots, GROUP * features)
     grads_t[...] = ordered.T.astype(jnp.bfloat16).reshape(GROUP, features, total)
 
-    for copy in weight_copies:
+    for copy in weight_copies[2:] + passed:
         copy.wait()
+    for copy in weight_copies[:2]:
+        copy.wait_send()
+    upper = depth // (GROUP // 2)
 
     def own_step(k, carry):
-        at = (depth + 2 + k) % GROUP
+        at = upper * k + (1 - upper) * (last - k)
         context_own[at] = jnp.dot(
             grads[at], weights[...].reshape(GROUP * features, -1),
             preferred_element_type=jnp.float32,
         )
         return carry
 
-    lax.fori_loop(0, GROUP, own_step, 0)
-
-    def sum_up(s):
-        return send(up_out.at[s], up_in.at[s], gu_send.at[s], gu_recv.at[s],
+
+    part_rows = slots // 2
+
+    def sum_up(s, h):
+        return send(up_out.at[s, h], up_in.at[s, h], gu_send.at[2 * s + h], gu_recv.at[2 * s + h],
                     ((depth + 1) * GROUP + plane, core))
 
-    def sum_down(s):
-        return send(down_out.at[s], down_in.at[s], gd_send.at[s], gd_recv.at[s],
-                    ((depth - 1) * GROUP + plane, core))
-
-    def up_wait(s):
-        send(up_in.at[s], up_in.at[s], gu_send.at[s], gu_recv.at[s], (e, other)).wait_recv()
-
-    def down_wait(s):
-        send(down_in.at[s], down_in.at[s], gd_send.at[s], gd_recv.at[s], (e, other)).wait_recv()
-
-    def sum_step(s):
+    def sum_down(s, h):
+        return send(down_out.at[s, h], down_in.at[s, h], gd_send.at[2 * s + h],
+                    gd_recv.at[2 * s + h], ((depth - 1) * GROUP + plane, core))
+
+    def up_wait(s, h):
+        ref = up_in.at[s, h]
+        send(ref, ref, gu_send.at[2 * s + h], gu_recv.at[2 * s + h], (e, other)).wait_recv()
+
+    def down_wait(s, h):
+        ref = down_in.at[s, h]
+        send(ref, ref, gd_send.at[2 * s + h], gd_recv.at[2 * s + h], (e, other)).wait_recv()
+
+    def sum_step(s, h):
+        piece = slice(h * part_rows, (h + 1) * part_rows)
+
         @pl.when((depth < last) & (depth <= s))
         def _():
             at = last + depth - s
             if s == 0:
-                up_out[s] = context_own[at].astype(jnp.bfloat16)
+                up_out[s, h] = context_own[at, piece].astype(jnp.bfloat16)
             else:
 
                 @pl.when(depth == 0)
                 def _():
-                    up_out[s] = context_own[at].astype(jnp.bfloat16)
+                    up_out[s, h] = context_own[at, piece].astype(jnp.bfloat16)
 
                 @pl.when(depth > 0)
                 def _():
-                    up_wait(s - 1)
-                    up_out[s] = (
-                        context_own[at] + up_in[s - 1].astype(jnp.float32)
+                    up_wait(s - 1, h)
+                    up_out[s, h] = (
+                        context_own[at, piece] + up_in[s - 1, h].astype(jnp.float32)
                     ).astype(jnp.bfloat16)
 
-            sum_up(s).start()
+            sum_up(s, h).start()
 
         @pl.when((depth > 0) & (last - depth <= s))
         def _():
             at = depth - last + s
             if s == 0:
-                down_out[s] = context_own[at].astype(jnp.bfloat16)
+                down_out[s, h] = context_own[at, piece].astype(jnp.bfloat16)
             else:
 
                 @pl.when(depth == last)
                 def _():
-                    down_out[s] = context_own[at].astype(jnp.bfloat16)
+                    down_out[s, h] = context_own[at, piece].astype(jnp.bfloat16)
 
                 @pl.when(depth < last)
                 def _():
-                    down_wait(s - 1)
-                    down_out[s] = (
-                        context_own[at] + down_in[s - 1].astype(jnp.float32)
+                    down_wait(s - 1, h)
+                    down_out[s, h] = (
+                        context_own[at, piece] + down_in[s - 1, h].astype(jnp.float32)
                     ).astype(jnp.bfloat16)
 
-            sum_down(s).start()
-
-    sum_step(0)
+            sum_down(s, h).start()
+
+    own_step(0, 0)
+    sum_step(0, 0)
+    sum_step(0, 1)
+    lax.fori_loop(1, GROUP, own_step, 0)
 
     context_wait(2)
 
@@ -310,8 +344,9 @@
         return carry
 
     lax.fori_loop(1, GROUP + 1, weight_step, 0)
-    sum_step(1)
-    sum_step(2)
+    for s in range(1, last):
+        for h in range(2):
+            sum_step(s, h)
 
     for k in range(1, GROUP):
         gw_copy(k).wait()
@@ -352,17 +387,20 @@
         copy.start()
     scale_ref[depth] = scale_group[...]
 
-    @pl.when(depth > 0)
-    def _():
-        up_wait(2)
-        context_own[depth] += up_in[2].astype(jnp.float32)
-
-    @pl.when(depth < last)
-    def _():
-        down_wait(2)
-        context_own[depth] += down_in[2].astype(jnp.float32)
-
-    grad_context_ref[...] = context_own[depth].astype(jnp.bfloat16)
+    for h in range(2):
+        piece = slice(h * part_rows, (h + 1) * part_rows)
+
+        @pl.when(depth > 0)
+        def _():
+            up_wait(last - 1, h)
+            context_own[depth, piece] += up_in[last - 1, h].astype(jnp.float32)
+
+        @pl.when(depth < last)
+        def _():
+            down_wait(last - 1, h)
+            context_own[depth, piece] += down_in[last - 1, h].astype(jnp.float32)
+
+        grad_context_ref[piece, :] = context_own[depth, piece].astype(jnp.bfloat16)
 
     for s in range(last):
 
@@ -376,11 +414,13 @@
 
         @pl.when((depth < last) & (depth <= s))
         def _():
-            sum_up(s).wait_send()
+            for h in range(2):
+                sum_up(s, h).wait_send()
 
         @pl.when((depth > 0) & (last - depth <= s))
         def _():
-            sum_down(s).wait_send()
+            for h in range(2):
+                sum_down(s, h).wait_send()
 
     for copy in all_copies:
         copy.wait()
@@ -402,9 +442,9 @@
     total = GROUP * slot_count
     bf16, f32 = jnp.bfloat16, jnp.float32
     small = up(padded, 128)
-    sems = [2, 3, 3, 3, 3, 3, 3, 7, 7, 3, 3, 3, 3, 3, 3, 3, 3, 3, 3, 7, 7, 3, 3]
+    sems = [6, 3, 3, 3, 3, 6, 6, 7, 7, 3, 3, 3, 3, 6, 6, 6, 6, 3, 3, 7, 7, 3, 3]
     vmem = pl.BlockSpec(memory_space=pltpu.VMEM)
-    far = pl.BlockSpec(memory_space=pl.ANY)
+    far = pl.BlockSpec(memory_space=pltpu.HBM)
     grad_context, grad_weight, scales = pl.pallas_call(
         functools.partial(kernel, capacity, rescale),
         out_shape=(
@@ -412,12 +452,16 @@
             jax.ShapeDtypeStruct((share, columns), f32),
             jax.ShapeDtypeStruct((GROUP, GROUP, 8, small), f32),
         ),
-        in_specs=[far, vmem, far, vmem, vmem, vmem],
+        in_specs=[far] * 6,
         out_specs=[vmem] * 3,
         scratch_shapes=[
             pltpu.VMEM((source_rows, features), bf16),
             pltpu.VMEM((source_rows, features), bf16),
             pltpu.VMEM((slot_count, columns), bf16),
+            pltpu.VMEM((1, source_rows), jnp.int32),
+            pltpu.VMEM((columns // BLOCK, slot_count), f32),
+            pltpu.VMEM((share, columns), bf16),
+            pltpu.VMEM((features,), f32),
             pltpu.VMEM((GROUP, source_rows, width), bf16),
             pltpu.VMEM((GROUP, 8, GROUP * source_rows), jnp.int32),
             pltpu.VMEM((GROUP, block, GROUP * padded), bf16),
@@ -427,10 +471,10 @@
             pltpu.VMEM((GROUP, slot_count, columns), bf16),
             pltpu.VMEM((GROUP, padded, columns), bf16),
             pltpu.VMEM((GROUP, slot_count, columns), f32),
-            pltpu.VMEM((GROUP - 1, slot_count, columns), bf16),
-            pltpu.VMEM((GROUP - 1, slot_count, columns), bf16),
-            pltpu.VMEM((GROUP - 1, slot_count, columns), bf16),
-            pltpu.VMEM((GROUP - 1, slot_count, columns), bf16),
+            pltpu.VMEM((GROUP - 1, 2, slot_count // 2, columns), bf16),
+            pltpu.VMEM((GROUP - 1, 2, slot_count // 2, columns), bf16),
+            pltpu.VMEM((GROUP - 1, 2, slot_count // 2, columns), bf16),
+            pltpu.VMEM((GROUP - 1, 2, slot_count // 2, columns), bf16),
             pltpu.VMEM((GROUP, padded, columns), bf16),
             pltpu.VMEM((GROUP, padded, columns), bf16),
             pltpu.VMEM((owners * GROUP, 8, small), f32),
@@ -438,9 +482,9 @@
         ]
         + [pltpu.SemaphoreType.DMA((n,)) for n in sems],
         compiler_params=pltpu.CompilerParams(
-            collective_id=0, has_side_effects=True, vmem_limit_bytes=48 * 2**20
+            collective_id=0, has_side_effects=True, vmem_limit_bytes=64 * 2**20
         ),
-    )(grad_rows, row_target.T, stored_context, block_scale.T, w_out.T, layer_scale[None, :])
+    )(grad_rows, row_target.T, stored_context, block_scale.T, w_out.T, layer_scale)
     grad_scale = scales[:, :, 0, :share].reshape(features) / layer_scale
     return (grad_context, grad_weight, grad_scale)
 

time: 79.2 us -> 77.2 us (0.975)
  Pallas kernels: 71.4 us -> 70.1 us
    pallas_call x1, Pallas kernels: 71.4 us -> 70.1 us  [two_level(): pl.pallas_call(functools.partial(kernel, capacity, rescale), out_shape=(j...]
    slice x1, local copies, waits for them, and re-layouts: 0.05 us -> 0.95 us  [two_level(): grad_scale = scales[:, :, 0, :share].reshape(features) / layer_scale]
    unnamed x14 -> x4, local copies, waits for them, and re-layouts: 5.19 us -> 4.44 us
where the time goes in v3:
time: 77.2 us; the launch traced here: 76.9 us
  Pallas kernels  70.1 us (91%)
  local copies, waits for them, and re-layouts  5.49 us (7%)
    pallas_call x1, Pallas kernels, two_level(): pl.pallas_call(functools.partial(kernel, capacity, rescale), out_shape=(j...  70.1 us
    unnamed x4, local copies, waits for them, and re-layouts  4.44 us

profile of v3, /device:TPU:0, one launch (start us, length us, event | category | flops | bytes accessed | tf_op | source)
XLA Modules:
  0.0 76.9 jit_solution(7253964868758546464)
XLA Ops:
  0.6 70.1 %shard_map.85 = (bf16[160,1024]{1,0:T(8,128)(2,1)}, f32[200,1024]{1,0:T(8,128)}, f32[4,4,8,256]{3,2,1,0:T(8,128)}) custom-call(bf16[64,3200]{1,0:T(8,128)(2,1)} %gradient_ref.1, s32[1,64]{1,0:T(1,128)} %bitcast.5, bf16[160,1024]{1,0:T(8,128)(2,1)} %stored_ref.1, f32[8,160]{1,0:T(8,128)} %bitcast.4, bf16[200,1024]{1,0:T(8,128)(2,1)} %bitcast.3, f32[3200]{0:T(1024)} %layer_in_ref.1), custom_call_target="tpu_custom_call" | custom-call | tf_op jit(solution)/shard_map/pallas_call | solution.py:448
  70.7 1.0 %slice_reduce_fusion = f32[4,4,200]{2,1,0:T(4,128)S(1)} fusion(f32[4,4,8,256]{3,2,1,0:T(8,128)} %get-tuple-element.8), kind=kLoop, calls=%fused_computation | loop fusion | bytes 25600 | tf_op jit(solution)/shard_map/slice | solution.py:488
  71.7 0.0 copy-start
  71.7 0.1 reshape_squeeze.3
  71.8 0.6 copy-done
  72.4 0.6 div.3
  73.0 1.7 %copy.11 = bf16[160,1024]{1,0:T(8,128)(2,1)} copy(bf16[160,1024]{1,0:T(8,128)(2,1)} %get-tuple-element.12) | data formatting | bytes 655360
  74.8 2.1 %copy.12 = f32[200,1024]{1,0:T(8,128)} copy(f32[200,1024]{1,0:T(8,128)} %get-tuple-element.13) | data formatting | bytes 1638400
Async XLA Ops:
  71.7 0.7 copy-start

commit v4 on v3

--- a/solution.py
+++ b/solution.py
@@ -21,8 +21,8 @@
     capacity, rescale, gradient_ref, target_ref, stored_ref, block_ref, weight_in_ref, layer_in_ref,
     grad_context_ref, grad_weight_ref, scale_ref,
     gradient, scaled, stored, targets, blocks, weight_own, layer, row_buf, place_buf, routed, arrived, grads, grads_t, contexts,
-    weights, context_own, up_out, up_in, down_out, down_in, weight_out, weight_in,
-    scale_plane, scale_group,
+    weights, context_own, up_out, up_in, down_out, down_in, weight_full, weight_out, weight_in,
+    scale_plane, scale_group, scale_all,
     load_sem, row_send, row_recv, place_send, place_recv, weight_send, weight_recv,
     routed_send, routed_recv, cu_send, cu_recv, cd_send, cd_recv, gu_send, gu_recv,
     gd_send, gd_recv, gw_send, gw_recv, plane_send, plane_recv, all_send, all_recv,
@@ -111,6 +111,7 @@
         copy.start()
     half = weights.shape[2] // 2
     beside = plane // 2 * 2 + (1 - plane % 2)
+    corner = last - plane
     across = (1 - plane // 2) * 2 + plane % 2
 
     def weight_copy(index, owner, part, to):
@@ -167,8 +168,6 @@
         @pl.when((depth > 0) & (depth + s <= last))
         def _():
             context_down(s).start()
-
-    context_step(0)
 
     lane = lax.broadcasted_iota(jnp.int32, (1, GROUP * features), 1)
     part = jnp.zeros_like(lane)
@@ -204,6 +203,7 @@
     choice = jnp.where(wanted == places, 1.0, 0.0).astype(jnp.bfloat16)
     for copy in row_copies:
         copy.wait()
+    context_step(0)
     owned = jnp.dot(
         row_buf[...].reshape(GROUP * source_rows, width), select,
         preferred_element_type=jnp.float32,
@@ -214,19 +214,16 @@
         .reshape(GROUP, block, GROUP * features)
     )
     mine = core * GROUP + plane
-    routed_copies = []
-    for k in range(1, GROUP):
-        for which, owner in enumerate((core, other)):
-            index = 2 * (k - 1) + which
-            routed_copies.append(
-                send(routed.at[ahead(plane, k)], arrived.at[mine],
-                     routed_send.at[index], routed_recv.at[index], along_plane(k, owner))
-            )
-    routed_copies.append(
-        send(routed.at[plane], arrived.at[mine], routed_send.at[2 * last],
-             routed_recv.at[2 * last], (e, other))
-    )
-    for copy in routed_copies:
+    routed_copies = [
+        send(routed.at[ahead(plane, k)], arrived.at[mine], routed_send.at[k - 1],
+             routed_recv.at[k - 1], along_plane(k, core))
+        for k in range(1, GROUP)
+    ]
+    shared_copies = [
+        send(routed.at[plane], arrived.at[mine], routed_send.at[last], routed_recv.at[last],
+             (e, other))
+    ]
+    for copy in routed_copies + shared_copies:
         copy.start()
     arrived[mine] = routed[plane]
     weight_copies[0].wait_recv()
@@ -234,15 +231,22 @@
     passed = [weight_copy(4, beside, 0, across), weight_copy(5, across, 1, beside)]
     for copy in passed:
         copy.start()
+    for k in range(1, GROUP):
+        routed_copies[k - 1].wait_recv()
+        block_at = arrived.at[core * GROUP + ahead(plane, GROUP - k)]
+        shared_copies.append(
+            send(block_at, block_at, routed_send.at[last + k], routed_recv.at[last + k], (e, other))
+        )
+        shared_copies[-1].start()
     context_step(1)
-    context_step(2)
+    for copy in shared_copies:
+        copy.wait()
     for copy in routed_copies:
-        copy.wait()
+        copy.wait_send()
     ordered = jnp.dot(
         order, arrived[...].reshape(total, GROUP * features), preferred_element_type=jnp.float32
     )
     grads[...] = ordered.astype(jnp.bfloat16).reshape(GROUP, slots, GROUP * features)
-    grads_t[...] = ordered.T.astype(jnp.bfloat16).reshape(GROUP, features, total)
 
     for copy in weight_copies[2:] + passed:
         copy.wait()
@@ -324,35 +328,59 @@
     sum_step(0, 0)
     sum_step(0, 1)
     lax.fori_loop(1, GROUP, own_step, 0)
+    context_step(2)
+    grads_t[...] = ordered.T.astype(jnp.bfloat16).reshape(GROUP, features, total)
+    sum_step(1, 0)
+    sum_step(1, 1)
 
     context_wait(2)
 
-    def gw_copy(k):
-        return send(weight_out.at[ahead(plane, k)], weight_in.at[plane],
-                    gw_send.at[k - 1], gw_recv.at[k - 1], along_plane(k, core))
-
-    def weight_step(k, carry):
-        at = ahead(plane, k)
-        weight_out[at] = jnp.dot(
+    def weight_step(at):
+        weight_full[at] = jnp.dot(
             grads_t[at], contexts[...].reshape(total, -1), preferred_element_type=jnp.float32
-        ).astype(jnp.bfloat16)
-
-        @pl.when(k < GROUP)
-        def _():
-            gw_copy(k).start()
-
-        return carry
-
-    lax.fori_loop(1, GROUP + 1, weight_step, 0)
-    for s in range(1, last):
-        for h in range(2):
-            sum_step(s, h)
-
-    for k in range(1, GROUP):
-        gw_copy(k).wait()
-    summed = weight_out[plane].astype(jnp.float32)
-    for k in range(1, GROUP):
-        summed = summed + weight_in[ahead(plane, GROUP - k)].astype(jnp.float32)
+        )
+
+    def columns_of(at, h):
+        return weight_full[at, :, h * half : (h + 1) * half]
+
+    def gw_copy(index, to):
+        return send(weight_out.at[index], weight_in.at[index], gw_send.at[index],
+                    gw_recv.at[index], (depth * GROUP + to, core))
+
+    gw_copies = [gw_copy(i, to) for i, to in enumerate((beside, across) * 2)]
+    gw_copies += [gw_copy(4, across), gw_copy(5, beside)]
+
+    def gw_start(index, value):
+        weight_out[index] = value.astype(jnp.bfloat16)
+        gw_copies[index].start()
+
+    weight_step(corner)
+    gw_start(0, columns_of(corner, 0))
+    gw_start(1, columns_of(corner, 1))
+    weight_step(beside)
+    gw_start(2, columns_of(beside, 0))
+    weight_step(across)
+    gw_start(3, columns_of(across, 1))
+    weight_step(plane)
+    gw_copies[0].wait_recv()
+    gw_start(4, columns_of(across, 0) + weight_in[0].astype(jnp.float32))
+    gw_copies[1].wait_recv()
+    gw_start(5, columns_of(beside, 1) + weight_in[1].astype(jnp.float32))
+    sum_step(2, 0)
+    sum_step(2, 1)
+    for index in (2, 3, 4, 5):
+        gw_copies[index].wait_recv()
+    for copy in gw_copies:
+        copy.wait_send()
+    summed = jnp.concatenate(
+        [
+            columns_of(plane, h)
+            + weight_in[2 + h].astype(jnp.float32)
+            + weight_in[4 + h].astype(jnp.float32)
+            for h in range(2)
+        ],
+        axis=1,
+    )
     product = summed * weights[plane].astype(jnp.float32)
     lanes = product[:, :BLOCK]
     for j in range(1, product.shape[1] // BLOCK):
@@ -379,13 +407,13 @@
     for j in range(GROUP):
         scale_group[j] = scale_plane[j] + scale_plane[GROUP + j]
     all_copies = [
-        send(scale_group, scale_ref.at[depth], all_send.at[k - 1], all_recv.at[k - 1],
+        send(scale_group, scale_all.at[depth], all_send.at[k - 1], all_recv.at[k - 1],
              along_depth(k))
         for k in range(1, GROUP)
     ]
     for copy in all_copies:
         copy.start()
-    scale_ref[depth] = scale_group[...]
+    scale_all[depth] = scale_group[...]
 
     for h in range(2):
         piece = slice(h * part_rows, (h + 1) * part_rows)
@@ -424,6 +452,10 @@
 
     for copy in all_copies:
         copy.wait()
+    whole = jnp.concatenate(
+        [scale_all[d, q, 0:1, :share] for d in range(GROUP) for q in range(GROUP)], axis=1
+    )
+    scale_ref[...] = (whole / layer[...].reshape(1, -1)).reshape(-1)
 
 
 def two_level(grad_rows, row_target, stored_context, block_scale, w_out, layer_scale):
@@ -442,15 +474,15 @@
     total = GROUP * slot_count
     bf16, f32 = jnp.bfloat16, jnp.float32
     small = up(padded, 128)
-    sems = [6, 3, 3, 3, 3, 6, 6, 7, 7, 3, 3, 3, 3, 6, 6, 6, 6, 3, 3, 7, 7, 3, 3]
+    sems = [6, 3, 3, 3, 3, 6, 6, 7, 7, 3, 3, 3, 3, 6, 6, 6, 6, 6, 6, 7, 7, 3, 3]
     vmem = pl.BlockSpec(memory_space=pltpu.VMEM)
     far = pl.BlockSpec(memory_space=pltpu.HBM)
-    grad_context, grad_weight, scales = pl.pallas_call(
+    return pl.pallas_call(
         functools.partial(kernel, capacity, rescale),
         out_shape=(
             jax.ShapeDtypeStruct((slot_count, columns), bf16),
             jax.ShapeDtypeStruct((share, columns), f32),
-            jax.ShapeDtypeStruct((GROUP, GROUP, 8, small), f32),
+            jax.ShapeDtypeStruct((features,), f32),
         ),
         in_specs=[far] * 6,
         out_specs=[vmem] * 3,
@@ -475,18 +507,18 @@
             pltpu.VMEM((GROUP - 1, 2, slot_count // 2, columns), bf16),
             pltpu.VMEM((GROUP - 1, 2, slot_count // 2, columns), bf16),
             pltpu.VMEM((GROUP - 1, 2, slot_count // 2, columns), bf16),
-            pltpu.VMEM((GROUP, padded, columns), bf16),
-            pltpu.VMEM((GROUP, padded, columns), bf16),
+            pltpu.VMEM((GROUP, padded, columns), f32),
+            pltpu.VMEM((6, padded, columns // 2), bf16),
+            pltpu.VMEM((6, padded, columns // 2), bf16),
             pltpu.VMEM((owners * GROUP, 8, small), f32),
             pltpu.VMEM((GROUP, 8, small), f32),
+            pltpu.VMEM((GROUP, GROUP, 8, small), f32),
         ]
         + [pltpu.SemaphoreType.DMA((n,)) for n in sems],
         compiler_params=pltpu.CompilerParams(
             collective_id=0, has_side_effects=True, vmem_limit_bytes=64 * 2**20
         ),
     )(grad_rows, row_target.T, stored_context, block_scale.T, w_out.T, layer_scale)
-    grad_scale = scales[:, :, 0, :share].reshape(features) / layer_scale
-    return (grad_context, grad_weight, grad_scale)
 
 
 def on_device(grad_rows, row_target, stored_context, block_scale, w_out, layer_scale):

time: 77.2 us -> 70.9 us (0.918)
  Pallas kernels: 70.1 us -> 65.6 us
  local copies, waits for them, and re-layouts: 5.49 us -> 4.46 us
    pallas_call x1, Pallas kernels: 70.1 us -> 65.6 us  [two_level(): pl.pallas_call(functools.partial(kernel, capacity, rescale), out_shape=(j...]
    slice x1 -> x0, local copies, waits for them, and re-layouts: 0.95 us -> none  [two_level(): grad_scale = scales[:, :, 0, :share].reshape(features) / layer_scale]
    unnamed x4 -> x5, local copies, waits for them, and re-layouts: 4.44 us -> 4.46 us
where the time goes in v4:
time: 70.9 us; the launch traced here: 70.7 us
  Pallas kernels  65.6 us (93%)
  local copies, waits for them, and re-layouts  4.46 us (6%)
    pallas_call x1, Pallas kernels, two_level(): pl.pallas_call(functools.partial(kernel, capacity, rescale), out_shape=(j...  65.6 us
    unnamed x5, local copies, waits for them, and re-layouts  4.46 us

profile of v4, /device:TPU:0, one launch (start us, length us, event | category | flops | bytes accessed | tf_op | source)
XLA Modules:
  0.0 70.7 jit_solution(8426571484723482921)
XLA Ops:
  0.6 65.6 %shard_map.85 = (bf16[160,1024]{1,0:T(8,128)(2,1)}, f32[200,1024]{1,0:T(8,128)}, f32[3200]{0:T(1024)}) custom-call(bf16[64,3200]{1,0:T(8,128)(2,1)} %gradient_ref.1, s32[1,64]{1,0:T(1,128)} %bitcast.5, bf16[160,1024]{1,0:T(8,128)(2,1)} %stored_ref.1, f32[8,160]{1,0:T(8,128)} %bitcast.4, bf16[200,1024]{1,0:T(8,128)(2,1)} %bitcast.3, f32[3200]{0:T(1024)} %layer_in_ref.1), custom_call_target="tpu_custom_call" | custom-call | tf_op jit(solution)/shard_map/pallas_call | solution.py:480
  66.2 1.7 %copy.12 = bf16[160,1024]{1,0:T(8,128)(2,1)} copy(bf16[160,1024]{1,0:T(8,128)(2,1)} %get-tuple-element.6) | data formatting | bytes 655360
  68.0 0.0 copy-start
  68.0 2.1 %copy.13 = f32[200,1024]{1,0:T(8,128)} copy(f32[200,1024]{1,0:T(8,128)} %get-tuple-element.7) | data formatting | bytes 1638400
  70.1 0.0 copy-done
  70.1 0.6 copy.14
Async XLA Ops:
  68.0 2.1 %copy-start = (f32[3200]{0:T(1024)S(1)}, f32[3200]{0:T(1024)}, u32[]{:S(2)}) copy-start(f32[3200]{0:T(1024)} %get-tuple-element.8) | copy-start | bytes 38404

commit v5 on v4

--- a/solution.py
+++ b/solution.py
@@ -169,6 +169,8 @@
         def _():
             context_down(s).start()
 
+    context_step(0)
+
     lane = lax.broadcasted_iota(jnp.int32, (1, GROUP * features), 1)
     part = jnp.zeros_like(lane)
     for k in range(1, GROUP):
@@ -194,6 +196,12 @@
     order = jnp.where(
         lax.broadcasted_iota(jnp.int32, (total, total), 1) == found, 1.0, 0.0
     ).astype(jnp.bfloat16)
+    weight_copies[0].wait_recv()
+    weight_copies[1].wait_recv()
+    passed = [weight_copy(4, beside, 0, across), weight_copy(5, across, 1, beside)]
+    for copy in passed:
+        copy.start()
+
     for copy in place_copies:
         copy.wait()
     places = place_buf[0, 0:1, :]
@@ -203,7 +211,6 @@
     choice = jnp.where(wanted == places, 1.0, 0.0).astype(jnp.bfloat16)
     for copy in row_copies:
         copy.wait()
-    context_step(0)
     owned = jnp.dot(
         row_buf[...].reshape(GROUP * source_rows, width), select,
         preferred_element_type=jnp.float32,
@@ -226,11 +233,7 @@
     for copy in routed_copies + shared_copies:
         copy.start()
     arrived[mine] = routed[plane]
-    weight_copies[0].wait_recv()
-    weight_copies[1].wait_recv()
-    passed = [weight_copy(4, beside, 0, across), weight_copy(5, across, 1, beside)]
-    for copy in passed:
-        copy.start()
+    context_step(1)
     for k in range(1, GROUP):
         routed_copies[k - 1].wait_recv()
         block_at = arrived.at[core * GROUP + ahead(plane, GROUP - k)]
@@ -238,7 +241,6 @@
             send(block_at, block_at, routed_send.at[last + k], routed_recv.at[last + k], (e, other))
         )
         shared_copies[-1].start()
-    context_step(1)
     for copy in shared_copies:
         copy.wait()
     for copy in routed_copies:
@@ -327,8 +329,8 @@
     own_step(0, 0)
     sum_step(0, 0)
     sum_step(0, 1)
+    context_step(2)
     lax.fori_loop(1, GROUP, own_step, 0)
-    context_step(2)
     grads_t[...] = ordered.T.astype(jnp.bfloat16).reshape(GROUP, features, total)
     sum_step(1, 0)
     sum_step(1, 1)
@@ -480,9 +482,9 @@
     return pl.pallas_call(
         functools.partial(kernel, capacity, rescale),
         out_shape=(
-            jax.ShapeDtypeStruct((slot_count, columns), bf16),
-            jax.ShapeDtypeStruct((share, columns), f32),
-            jax.ShapeDtypeStruct((features,), f32),
+            pltpu.VMEM((slot_count, columns), bf16),
+            pltpu.VMEM((share, columns), f32),
+            pltpu.VMEM((features,), f32),
         ),
         in_specs=[far] * 6,
         out_specs=[vmem] * 3,
@@ -516,9 +518,16 @@
         ]
         + [pltpu.SemaphoreType.DMA((n,)) for n in sems],
         compiler_params=pltpu.CompilerParams(
-            collective_id=0, has_side_effects=True, vmem_limit_bytes=64 * 2**20
+            collective_id=0, has_side_effects=True, vmem_limit_bytes=48 * 2**20
         ),
-    )(grad_rows, row_target.T, stored_context, block_scale.T, w_out.T, layer_scale)
+    )(
+        *[
+            pltpu.with_memory_space_constraint(array, pltpu.HBM)
+            for array in (
+                grad_rows, row_target.T, stored_context, block_scale.T, w_out.T, layer_scale
+            )
+        ]
+    )
 
 
 def on_device(grad_rows, row_target, stored_context, block_scale, w_out, layer_scale):

time: 70.9 us -> 67.9 us (0.958)
  local copies, waits for them, and re-layouts: 4.46 us -> 2.22 us
    unnamed x5 -> x3, local copies, waits for them, and re-layouts: 4.46 us -> 2.22 us
where the time goes in v5:
time: 67.9 us; the launch traced here: 67.8 us
  Pallas kernels  64.9 us (96%)
  local copies, waits for them, and re-layouts  2.22 us (3%)
    pallas_call x1, Pallas kernels, two_level(): pl.pallas_call(functools.partial(kernel, capacity, rescale), out_shape=(p...  64.9 us
    unnamed x3, local copies, waits for them, and re-layouts  2.22 us

profile of v5, /device:TPU:0, one launch (start us, length us, event | category | flops | bytes accessed | tf_op | source)
XLA Modules:
  0.0 67.8 jit_solution(6857007076546302452)
XLA Ops:
  0.6 64.9 %shard_map.85 = (bf16[160,1024]{1,0:T(8,128)(2,1)S(1)}, f32[200,1024]{1,0:T(8,128)S(1)}, f32[3200]{0:T(1024)S(1)}) custom-call(bf16[64,3200]{1,0:T(8,128)(2,1)} %gradient_ref.1, s32[1,64]{1,0:T(1,128)} %bitcast.5, bf16[160,1024]{1,0:T(8,128)(2,1)} %stored_ref.1, f32[8,160]{1,0:T(8,128)} %bitcast.4, bf16[200,1024]{1,0:T(8,128)(2,1)} %bitcast.3, f32[3200]{0:T(1024)} %layer_in_ref.1), custom_call_target="tpu_custom_call" | custom-call | tf_op jit(solution)/shard_map/pallas_call | solution.py:482
  65.6 0.7 %copy.12 = bf16[160,1024]{1,0:T(8,128)(2,1)} copy(bf16[160,1024]{1,0:T(8,128)(2,1)S(1)} %get-tuple-element.3) | data formatting | bytes 655360
  66.3 0.6 copy.14
  66.9 0.9 %copy.13 = f32[200,1024]{1,0:T(8,128)} copy(f32[200,1024]{1,0:T(8,128)S(1)} %get-tuple-element.4) | data formatting | bytes 1638400

commit v6 on v5

--- a/solution.py
+++ b/solution.py
@@ -249,6 +249,7 @@
         order, arrived[...].reshape(total, GROUP * features), preferred_element_type=jnp.float32
     )
     grads[...] = ordered.astype(jnp.bfloat16).reshape(GROUP, slots, GROUP * features)
+    context_step(2)
 
     for copy in weight_copies[2:] + passed:
         copy.wait()
@@ -329,11 +330,8 @@
     own_step(0, 0)
     sum_step(0, 0)
     sum_step(0, 1)
-    context_step(2)
     lax.fori_loop(1, GROUP, own_step, 0)
     grads_t[...] = ordered.T.astype(jnp.bfloat16).reshape(GROUP, features, total)
-    sum_step(1, 0)
-    sum_step(1, 1)
 
     context_wait(2)
 
@@ -364,6 +362,8 @@
     weight_step(across)
     gw_start(3, columns_of(across, 1))
     weight_step(plane)
+    sum_step(1, 0)
+    sum_step(1, 1)
     gw_copies[0].wait_recv()
     gw_start(4, columns_of(across, 0) + weight_in[0].astype(jnp.float32))
     gw_copies[1].wait_recv()

time: 67.9 us -> 67.2 us (0.990)
  Pallas kernels: 64.9 us -> 64.2 us
    pallas_call x1, Pallas kernels: 64.9 us -> 64.2 us  [two_level(): pl.pallas_call(functools.partial(kernel, capacity, rescale), out_shape=(p...]
where the time goes in v6:
time: 67.2 us; the launch traced here: 67.1 us
  Pallas kernels  64.2 us (96%)
  local copies, waits for them, and re-layouts  2.22 us (3%)
    pallas_call x1, Pallas kernels, two_level(): pl.pallas_call(functools.partial(kernel, capacity, rescale), out_shape=(p...  64.2 us
    unnamed x3, local copies, waits for them, and re-layouts  2.22 us

profile of v6, /device:TPU:0, one launch (start us, length us, event | category | flops | bytes accessed | tf_op | source)
XLA Modules:
  0.0 67.1 jit_solution(3115067256655106142)
XLA Ops:
  0.6 64.2 %shard_map.85 = (bf16[160,1024]{1,0:T(8,128)(2,1)S(1)}, f32[200,1024]{1,0:T(8,128)S(1)}, f32[3200]{0:T(1024)S(1)}) custom-call(bf16[64,3200]{1,0:T(8,128)(2,1)} %gradient_ref.1, s32[1,64]{1,0:T(1,128)} %bitcast.5, bf16[160,1024]{1,0:T(8,128)(2,1)} %stored_ref.1, f32[8,160]{1,0:T(8,128)} %bitcast.4, bf16[200,1024]{1,0:T(8,128)(2,1)} %bitcast.3, f32[3200]{0:T(1024)} %layer_in_ref.1), custom_call_target="tpu_custom_call" | custom-call | tf_op jit(solution)/shard_map/pallas_call | solution.py:482
  64.8 0.7 %copy.12 = bf16[160,1024]{1,0:T(8,128)(2,1)} copy(bf16[160,1024]{1,0:T(8,128)(2,1)S(1)} %get-tuple-element.3) | data formatting | bytes 655360
  65.6 0.6 copy.14
  66.2 0.9 %copy.13 = f32[200,1024]{1,0:T(8,128)} copy(f32[200,1024]{1,0:T(8,128)S(1)} %get-tuple-element.4) | data formatting | bytes 1638400

commit v7 on v6

--- a/solution.py
+++ b/solution.py
@@ -330,7 +330,6 @@
     own_step(0, 0)
     sum_step(0, 0)
     sum_step(0, 1)
-    lax.fori_loop(1, GROUP, own_step, 0)
     grads_t[...] = ordered.T.astype(jnp.bfloat16).reshape(GROUP, features, total)
 
     context_wait(2)
@@ -361,9 +360,10 @@
     gw_start(2, columns_of(beside, 0))
     weight_step(across)
     gw_start(3, columns_of(across, 1))
-    weight_step(plane)
+    lax.fori_loop(1, GROUP, own_step, 0)
     sum_step(1, 0)
     sum_step(1, 1)
+    weight_step(plane)
     gw_copies[0].wait_recv()
     gw_start(4, columns_of(across, 0) + weight_in[0].astype(jnp.float32))
     gw_copies[1].wait_recv()

time: 67.2 us -> 67.2 us (level)
  no operation moved by 1% of the time
where the time goes in v7:
time: 67.2 us; the launch traced here: 67 us
  Pallas kernels  64.2 us (96%)
  local copies, waits for them, and re-layouts  2.22 us (3%)
    pallas_call x1, Pallas kernels, two_level(): pl.pallas_call(functools.partial(kernel, capacity, rescale), out_shape=(p...  64.2 us
    unnamed x3, local copies, waits for them, and re-layouts  2.22 us

profile of v7, /device:TPU:0, one launch (start us, length us, event | category | flops | bytes accessed | tf_op | source)
XLA Modules:
  0.0 67.0 jit_solution(3818261451097403175)
XLA Ops:
  0.6 64.2 %shard_map.85 = (bf16[160,1024]{1,0:T(8,128)(2,1)S(1)}, f32[200,1024]{1,0:T(8,128)S(1)}, f32[3200]{0:T(1024)S(1)}) custom-call(bf16[64,3200]{1,0:T(8,128)(2,1)} %gradient_ref.1, s32[1,64]{1,0:T(1,128)} %bitcast.5, bf16[160,1024]{1,0:T(8,128)(2,1)} %stored_ref.1, f32[8,160]{1,0:T(8,128)} %bitcast.4, bf16[200,1024]{1,0:T(8,128)(2,1)} %bitcast.3, f32[3200]{0:T(1024)} %layer_in_ref.1), custom_call_target="tpu_custom_call" | custom-call | tf_op jit(solution)/shard_map/pallas_call | solution.py:482
  64.8 0.7 %copy.12 = bf16[160,1024]{1,0:T(8,128)(2,1)} copy(bf16[160,1024]{1,0:T(8,128)(2,1)S(1)} %get-tuple-element.3) | data formatting | bytes 655360
  65.5 0.6 copy.14
  66.2 0.9 %copy.13 = f32[200,1024]{1,0:T(8,128)} copy(f32[200,1024]{1,0:T(8,128)S(1)} %get-tuple-element.4) | data formatting | bytes 1638400
